TPU v7x, 32 devices: a whole 2x2x4 slice. The times are simulated.
32 devices in a mesh: section: 2 (over x), tok: 4 (over z), mdl: 4 (over y, core).
Axes of the slice: x: 2, y: 2, z: 4, core: 2. Of those that a mesh axis runs over, the one named last changes fastest.
Arguments:
- layer_input: bfloat16 [2, 1024, 2048], P(None, 'tok'), may hold values from -6 to 6
- segment_ids: int32 [2, 1024], replicated, may hold values from 0 to 3, as said below
- route_ids: int32 [2, 1024, 6], P(None, ('tok', 'mdl')), may hold values from 0 to 15, all different within a row; in each aligned block of 64 rows (0 to 63, 64 to 127, ..., all dimensions but the last counted through in order) at most 36 rows name the same one
- route_weights: float32 [2, 1024, 6], P(None, ('tok', 'mdl')), may hold values from 0.1 to 0.5
- attn_gain: float32 [2048], replicated, may hold values from 0.5 to 1.5
- w_query: bfloat16 [2048, 3072], P(None, 'mdl'), may hold values from -6.629126 to 6.629126
- w_kv_down: bfloat16 [2048, 576], replicated, may hold values from -0.13258252 to 0.13258252
- latent_gain: float32 [512], replicated, may hold values from 0.5 to 1.5
- w_kv_up: bfloat16 [512, 4096], P(None, 'mdl'), may hold values from -0.25 to 0.25
- w_out: bfloat16 [2048, 2048], P('mdl'), may hold values from -0.125 to 0.125
- ffn_gain: float32 [2048], replicated, may hold values from 0.5 to 1.5
- w_shared_gate: bfloat16 [2048, 2048], P(None, 'mdl'), may hold values from -0.125 to 0.125
- w_shared_up: bfloat16 [2048, 2048], P(None, 'mdl'), may hold values from -0.125 to 0.125
- w_shared_down: bfloat16 [2048, 2048], P('mdl'), may hold values from -0.125 to 0.125
- w_expert_gate: bfloat16 [16, 2048, 768], P(('tok', 'mdl')), may hold values from -0.125 to 0.125
- w_expert_up: bfloat16 [16, 2048, 768], P(('tok', 'mdl')), may hold values from -0.125 to 0.125
- w_expert_down: bfloat16 [16, 768, 2048], P(('tok', 'mdl')), may hold values from -0.21875 to 0.21875
Outputs:
- layer_output: bfloat16 [2, 1024, 2048], P('section', ('tok', 'mdl'))
Inputs may be any that keep to these rules, and one draw needn't show every extreme that they name: `segment_ids`: segment numbers never fall along a pack; each segment has 1 to 512 tokens and one has exactly 512. `route_ids`: each token names 6 different experts. In each aligned block of 64 tokens of a pack (the tokens of one device), no expert is named by more than 36 tokens, a bound that some block reaches.
All inputs are finite; a program needn't handle non-finite values.
Results may differ from a plain program's by a relative error of at most 0.02.
Values may be sent and summed in bfloat16 or wider, within the bound.
A program may use at most 128 MiB of HBM per device.

v0:
```python
import math

import jax
import jax.numpy as jnp
from jax import lax
from jax.sharding import PartitionSpec as P

NOPE = 128
ROPE = 64
VDIM = 128
LATENT = 512
SEGS = 4


EPS = 1e-06


def passed_along(value, axis, steps):
    count = lax.axis_size(axis)
    initial, last = (max(0, -steps), min(count, count - steps))
    return lax.ppermute(value, axis, [(source, source + steps) for source in range(initial, last)])


def rms_scale(values, gain_vec):
    values = values.astype(jnp.float32)
    return values * lax.rsqrt(jnp.mean(values * values, axis=-1, keepdims=True) + EPS) * gain_vec


def rotary(values, positions):
    half_width = values.shape[-1] // 2
    frequency = 10000.0 ** (-jnp.arange(half_width, dtype=jnp.float32) / half_width)
    angles = positions.astype(jnp.float32)[:, None] * frequency[None, :]
    if values.ndim == 3:
        angles = angles[:, None, :]
    cosine = jnp.cos(angles)
    sine_part = jnp.sin(angles)
    lead_half = values[..., :half_width]
    tail_half = values[..., half_width:]
    return jnp.concatenate(
        [lead_half * cosine - tail_half * sine_part, lead_half * sine_part + tail_half * cosine],
        axis=-1,
    )


def positions_of(segment_row, segment_count):
    labels = jnp.arange(segment_count, dtype=jnp.int32)
    starts = jnp.sum((segment_row[None, :] < labels[:, None]).astype(jnp.int32), axis=1)
    member = (segment_row[:, None] == labels[None, :]).astype(jnp.int32)
    return jnp.arange(segment_row.shape[0], dtype=jnp.int32) - jnp.sum(
        member * starts[None, :], axis=1
    )


def shards(
    layer_input,
    segment_ids,
    route_ids,
    route_weights,
    attn_gain,
    w_query,
    w_kv_down,
    latent_gain,
    w_kv_up,
    w_out,
    ffn_gain,
    w_shared_gate,
    w_shared_up,
    w_shared_down,
    w_expert_gate,
    w_expert_up,
    w_expert_down,
):
    n_mdl = lax.axis_size("mdl")
    n_wide = lax.axis_size(("tok", "mdl"))
    section_id = lax.axis_index("section")
    attending = section_id == 0
    expert_side = section_id == 1
    tok_rank = lax.axis_index("tok")
    mdl_rank = lax.axis_index("mdl")
    micro_count, tok_dev, model_width = layer_input.shape
    row_dev = tok_dev // n_mdl
    top_count = route_ids.shape[2]
    local_heads = w_out.shape[0] // VDIM
    qk_width = NOPE + ROPE
    score_scale = 1.0 / math.sqrt(qk_width)
    expert_dev = w_expert_gate.shape[0]
    expert_total = expert_dev * n_wide
    capacity = max(2, 3 * row_dev * top_count // (2 * expert_total))
    slot_total = expert_total * capacity
    slot_ids = jnp.arange(slot_total, dtype=jnp.int32)
    expert_labels = jnp.arange(expert_total, dtype=jnp.int32)
    results = []
    for batch_idx in range(micro_count):
        segment_row = segment_ids[batch_idx]
        positions = positions_of(segment_row, SEGS)
        query_start = tok_rank * tok_dev
        own_start = query_start + mdl_rank * row_dev
        query_pos = lax.dynamic_slice_in_dim(positions, query_start, tok_dev)
        own_pos = lax.dynamic_slice_in_dim(positions, own_start, row_dev)
        query_seg = lax.dynamic_slice_in_dim(segment_row, query_start, tok_dev)
        query_index = query_start + jnp.arange(tok_dev, dtype=jnp.int32)
        rows_in = layer_input[batch_idx]

        def project():
            normed = rms_scale(rows_in, attn_gain).astype(jnp.bfloat16)
            queries = jnp.dot(normed, w_query, preferred_element_type=jnp.float32).reshape(
                tok_dev, local_heads, qk_width
            )
            queries = jnp.concatenate(
                [queries[..., :NOPE], rotary(queries[..., NOPE:], query_pos)], axis=-1
            ).astype(jnp.bfloat16)
            own_normed = lax.dynamic_slice_in_dim(normed, mdl_rank * row_dev, row_dev)
            compressed = jnp.dot(own_normed, w_kv_down, preferred_element_type=jnp.float32)
            latent = rms_scale(compressed[:, :LATENT], latent_gain).astype(jnp.bfloat16)
            key_rope = rotary(compressed[:, LATENT:], own_pos).astype(jnp.bfloat16)
            return (queries, latent, key_rope)

        def no_project():
            return (
                jnp.zeros((tok_dev, local_heads, qk_width), jnp.bfloat16),
                jnp.zeros((row_dev, LATENT), jnp.bfloat16),
                jnp.zeros((row_dev, ROPE), jnp.bfloat16),
            )

        queries, latent, key_rope = lax.cond(attending, project, no_project)
        initial = (
            jnp.full((tok_dev, local_heads), -1e30, jnp.float32),
            jnp.zeros((tok_dev, local_heads), jnp.float32),
            jnp.zeros((tok_dev, local_heads, VDIM), jnp.float32),
        )
        latent_rows, rope_rows = (
            lax.all_gather(latent, "mdl", axis=0, tiled=True),
            lax.all_gather(key_rope, "mdl", axis=0, tiled=True),
        )
        expanded_here = (
            jnp.dot(latent_rows, w_kv_up, preferred_element_type=jnp.float32)
            .astype(jnp.bfloat16)
            .reshape(tok_dev, local_heads, NOPE + VDIM)
        )
        carried = initial
        expanded = lax.all_gather(expanded_here, "tok", axis=0, tiled=True)
        rope_keys = lax.all_gather(rope_rows, "tok", axis=0, tiled=True)
        key_count = expanded.shape[0]
        block_len = math.gcd(key_count, 512)
        block_count = key_count // block_len
        expanded_blocks = expanded.reshape(block_count, block_len, local_heads, NOPE + VDIM)
        rope_blocks = rope_keys.reshape(block_count, block_len, ROPE)

        def one_block(state_now, inputs):
            block_idx, kv_block, rope_block = inputs
            key_start = block_idx * block_len
            key_seg = lax.dynamic_slice_in_dim(segment_row, key_start, block_len)

            def update(state_old):
                running_max, totals, weighted = state_old
                scores = jnp.einsum(
                    "qhd,khd->qhk",
                    queries[..., :NOPE],
                    kv_block[..., :NOPE],
                    preferred_element_type=jnp.float32,
                )
                scores = scores + jnp.einsum(
                    "qhd,kd->qhk",
                    queries[..., NOPE:],
                    rope_block,
                    preferred_element_type=jnp.float32,
                )
                scores = scores * score_scale
                key_index = key_start + jnp.arange(block_len, dtype=jnp.int32)
                allowed = (key_seg[None, :] == query_seg[:, None]) & (
                    key_index[None, :] <= query_index[:, None]
                )
                allowed = allowed[:, None, :]
                masked = jnp.where(allowed, scores, -1e30)
                new_max = jnp.maximum(running_max, jnp.max(masked, axis=-1))
                weights = jnp.where(allowed, jnp.exp(scores - new_max[..., None]), 0.0)
                factor = jnp.exp(running_max - new_max)
                totals = totals * factor + jnp.sum(weights, axis=-1)
                weighted = weighted * factor[..., None] + jnp.einsum(
                    "qhk,khd->qhd",
                    weights.astype(jnp.bfloat16),
                    kv_block[..., NOPE:],
                    preferred_element_type=jnp.float32,
                )
                return (new_max, totals, weighted)

            def keep_state(state_old):
                return state_old

            return (lax.cond(attending, update, keep_state, state_now), None)

        carried, unused = lax.scan(
            one_block,
            carried,
            (jnp.arange(block_count, dtype=jnp.int32), expanded_blocks, rope_blocks),
        )
        running_max, totals, weighted = carried
        safe_totals = jnp.where(attending, totals, 1.0)
        attended = (
            (weighted / safe_totals[..., None])
            .astype(jnp.bfloat16)
            .reshape(tok_dev, local_heads * VDIM)
        )
        mixed_heads = lax.psum_scatter(
            jnp.dot(attended, w_out, preferred_element_type=jnp.float32).astype(jnp.bfloat16),
            "mdl",
            scatter_dimension=0,
            tiled=True,
        ).astype(jnp.float32)
        own_input = lax.dynamic_slice_in_dim(rows_in, mdl_rank * row_dev, row_dev)
        residual = (own_input.astype(jnp.float32) + mixed_heads).astype(jnp.bfloat16)
        arrived = passed_along(residual, "section", 1)
        normed_ffn = rms_scale(arrived, ffn_gain).astype(jnp.bfloat16)
        shard_rows = lax.all_gather(normed_ffn, "mdl", axis=0, tiled=True)

        def shared_compute():
            gate_proj = jnp.dot(shard_rows, w_shared_gate, preferred_element_type=jnp.float32)
            up_proj = jnp.dot(shard_rows, w_shared_up, preferred_element_type=jnp.float32)
            return (jax.nn.silu(gate_proj) * up_proj).astype(jnp.bfloat16)

        def shared_no_compute():
            return jnp.zeros((shard_rows.shape[0], w_shared_gate.shape[1]), jnp.bfloat16)

        shared_act = lax.cond(expert_side, shared_compute, shared_no_compute)
        shared_out = lax.psum_scatter(
            jnp.dot(shared_act, w_shared_down, preferred_element_type=jnp.float32).astype(
                jnp.bfloat16
            ),
            "mdl",
            scatter_dimension=0,
            tiled=True,
        ).astype(jnp.float32)
        expert_ids = route_ids[batch_idx].reshape(-1)
        onehot = (expert_ids[:, None] == expert_labels[None, :]).astype(jnp.int32)
        earlier = jnp.cumsum(onehot, axis=0) - onehot
        slot_index = jnp.sum(earlier * onehot, axis=1)
        target = expert_ids * capacity + slot_index
        placing = (
            (slot_ids[:, None] == target[None, :])
            .astype(jnp.int32)
            .reshape(slot_total, row_dev, top_count)
        )
        placing = jnp.sum(placing, axis=2).astype(jnp.bfloat16)
        outgoing = (
            jnp.dot(placing, normed_ffn, preferred_element_type=jnp.float32)
            .astype(jnp.bfloat16)
            .reshape(expert_total, capacity, model_width)
        )
        buffer = lax.all_to_all(outgoing, ("tok", "mdl"), split_axis=0, concat_axis=0, tiled=True)
        item_count = buffer.shape[1]
        grouped = (
            buffer.reshape(n_wide, expert_dev, item_count, model_width)
            .transpose(1, 0, 2, 3)
            .reshape(expert_dev, n_wide * item_count, model_width)
        )

        def run_compute():
            gate_proj = jnp.einsum(
                "erd,edf->erf", grouped, w_expert_gate, preferred_element_type=jnp.float32
            )
            up_proj = jnp.einsum(
                "erd,edf->erf", grouped, w_expert_up, preferred_element_type=jnp.float32
            )
            expert_act = (jax.nn.silu(gate_proj) * up_proj).astype(jnp.bfloat16)
            return jnp.einsum(
                "erf,efd->erd", expert_act, w_expert_down, preferred_element_type=jnp.float32
            ).astype(jnp.bfloat16)

        def run_no_compute():
            return jnp.zeros_like(grouped)

        produced = lax.cond(expert_side, run_compute, run_no_compute)
        processed = (
            produced.reshape(expert_dev, n_wide, item_count, model_width)
            .transpose(1, 0, 2, 3)
            .reshape(n_wide * expert_dev, item_count, model_width)
        )
        returned = lax.all_to_all(
            processed, ("tok", "mdl"), split_axis=0, concat_axis=0, tiled=True
        )
        weight_rows = route_weights[batch_idx]
        matched = target.reshape(row_dev, top_count)[:, :, None] == slot_ids[None, None, :]
        combining = jnp.sum(jnp.where(matched, weight_rows[:, :, None], 0.0), axis=1)
        routed = jnp.dot(
            combining,
            returned.reshape(slot_total, model_width).astype(jnp.float32),
            precision=lax.Precision.HIGHEST,
        )
        finished = (arrived.astype(jnp.float32) + shared_out + routed).astype(jnp.bfloat16)
        results.append(finished)
    half_count = micro_count // 2
    early_out = jnp.stack(results[:half_count])
    late_out = jnp.stack(results[half_count:])
    sent_back = passed_along(early_out, "section", -1)
    return jnp.where(attending, sent_back, late_out)


def solution(mesh):
    in_specs = (
        P(None, "tok", None),
        P(),
        P(None, ("tok", "mdl"), None),
        P(None, ("tok", "mdl"), None),
        P(),
        P(None, "mdl"),
        P(),
        P(),
        P(None, "mdl"),
        P("mdl", None),
        P(),
        P(None, "mdl"),
        P(None, "mdl"),
        P("mdl", None),
        P(("tok", "mdl"), None, None),
        P(("tok", "mdl"), None, None),
        P(("tok", "mdl"), None, None),
    )
    out_specs = P("section", ("tok", "mdl"), None)
    return jax.shard_map(shards, mesh=mesh, in_specs=in_specs, out_specs=out_specs, check_vma=False)
```

profile of v0, /device:TPU:0, one launch (start us, length us, event | category | flops | bytes accessed | tf_op | source)
XLA Modules:
  0.0 484.8 jit_solution(16630199862213393632)
XLA Ops:
  8.0 3.2 fusion.155
  11.3 15.8 %conditional.8 = (bf16[64,512]{1,0:T(8,128)(2,1)}, bf16[64,64]{0,1:T(8,128)(2,1)}, bf16[256,4,192]{2,0,1:T(8,128)(2,1)}) conditional(s32[]{:T(128)} %convert_element_type.246, () %tuple.95, (bf16[1,256,2048]{2,1,0:T(8,128)(2,1)}, f32[2048]{0:T(1024)S(1)}, bf16[2048,768]{1,0:T(8,128)(2,1)}, s32[1024]{0:T(1024)S(1)}, s32[1024,4]{0,1:T(4,128)S(1)}, ...), branch_computations={%region_0.0_spmd, %region_1.6_spmd} | conditional | flops 962554560 | bytes 31088918 | solution.py:125
  17.5 4.8 copy.146
  22.3 3.3 fusion.11
  27.0 7.5 %all_gather.30 = bf16[256,512]{1,0:T(8,128)(2,1)S(1)} all-gather(bf16[64,512]{1,0:T(8,128)(2,1)} %get-tuple-element.591), channel_id=1, replica_groups=mesh['section'=2,'tok'=4,'mdl'=4] {'mdl'}, dimensions={0}, use_global_device_ids=true | all-gather | bytes 327680 | tf_op jit(solution)/shard_map/all_gather | solution.py:132
  36.0 13.6 %conditional.11 = (bf16[64,512]{1,0:T(8,128)(2,1)S(1)}, bf16[64,64]{0,1:T(8,128)(2,1)S(1)}, bf16[256,4,192]{2,0,1:T(8,128)(2,1)S(1)}) conditional(s32[]{:T(128)} %convert_element_type.246, () %tuple.102, (bf16[1,256,2048]{2,1,0:T(8,128)(2,1)}, f32[2048]{0:T(1024)S(1)}, bf16[2048,768]{1,0:T(8,128)(2,1)}, s32[1024]{0:T(1024)S(1)}, ...), branch_computations={%region_24.25_spmd, %region_25.30_spmd} | conditional | flops 962554560 | bytes 35283248 | solution.py:125
  41.0 4.9 %copy.161 = bf16[2048,768]{0,1:T(8,128)(2,1)} copy(bf16[2048,768]{1,0:T(8,128)(2,1)} %get-tuple-element.877) | data formatting | bytes 6291456 | tf_op jit(solution)/shard_map
  45.9 3.0 fusion.68
  49.5 5.9 %all_gather.35 = bf16[256,512]{1,0:T(8,128)(2,1)S(1)} all-gather(bf16[64,512]{1,0:T(8,128)(2,1)S(1)} %get-tuple-element.596), channel_id=1, replica_groups=mesh['section'=2,'tok'=4,'mdl'=4] {'mdl'}, dimensions={0}, use_global_device_ids=true | all-gather | bytes 327680 | tf_op jit(solution)/shard_map/all_gather | solution.py:132
  58.8 5.2 %all_gather.32 = bf16[256,64]{1,0:T(8,128)(2,1)S(1)} all-gather(bf16[64,64]{1,0:T(8,128)(2,1)S(1)} %copy.149), channel_id=1, replica_groups=mesh['section'=2,'tok'=4,'mdl'=4] {'mdl'}, dimensions={0}, use_global_device_ids=true | all-gather | bytes 40960 | tf_op jit(solution)/shard_map/all_gather | solution.py:133
  64.1 16.9 %all_gather.33 = bf16[1024,64]{1,0:T(8,128)(2,1)S(1)} all-gather(bf16[256,64]{1,0:T(8,128)(2,1)S(1)} %all_gather.32), channel_id=1, replica_groups=mesh['section'=2,'tok'=4,'mdl'=4] {'tok'}, dimensions={0}, use_global_device_ids=true | all-gather | bytes 163840 | tf_op jit(solution)/shard_map/all_gather | solution.py:142
  81.2 5.3 %all-gather.5.cloned.1.call-done = bf16[1024,4,256]{2,0,1:T(8,128)(2,1)} async-done(((bf16[256,4,256]{2,0,1:T(8,128)(2,1)}), bf16[1024,4,256]{2,0,1:T(8,128)(2,1)}) %all-gather.5.cloned.1.call-update) | async-done | bytes 2097168 | tf_op jit(solution)/shard_map/all_gather | solution.py:141
  86.4 3.0 copy.151
  90.3 26.0 %while.30 = (s32[]{:T(128)}, f32[256,4]{0,1:T(4,128)S(1)}, f32[256,4]{0,1:T(4,128)S(1)}, f32[256,4,128]{2,0,1:T(8,128)}, pred[]{:T(512)}, /*index=5*/s32[1024]{0...) while((s32[]{:T(128)}, f32[256,4]{0,1:T(4,128)S(1)}, ...), condition=%wide.region_11.12_spmd.clone, body=%wide.region_6.11_spmd.clone.sunk | while | flops 341445376 | bytes 16531300 | solution.py:192
  90.3 13.0 %conditional.18 = ((f32[256,4]{0,1:T(4,128)S(1)}, f32[256,4]{0,1:T(4,128)S(1)}, f32[256,4,128]{2,0,1:T(8,128)})) conditional(s32[]{:T(128)} %convert_element_type.424, (f32[256,4]{0,1:T(4,128)S(1)}, f32[256,4]{0,1:T(4,128)S(1)}, f32[256,4,128]{2,0,1:T(8,128)}) %tuple.180, (s32[2]{0:T(128)S(1)}, s32[]{:T(128)}, s32[1024]{0:T(1024)S(1)}, ...), branch_computations={%region_7.7_spmd, %region_8.10_spmd} | conditional | flops 341445376 | bytes 16530026 | solution.py:190
  93.3 2.7 fusion.39
  96.0 2.0 copy.140
  98.1 2.3 select_reduce_fusion.1
  100.7 2.6 fusion.33
  103.3 13.0 %conditional.18 = ((f32[256,4]{0,1:T(4,128)S(1)}, f32[256,4]{0,1:T(4,128)S(1)}, f32[256,4,128]{2,0,1:T(8,128)})) conditional(s32[]{:T(128)} %convert_element_type.424, (f32[256,4]{0,1:T(4,128)S(1)}, f32[256,4]{0,1:T(4,128)S(1)}, f32[256,4,128]{2,0,1:T(8,128)}) %tuple.180, (s32[2]{0:T(128)S(1)}, s32[]{:T(128)}, s32[1024]{0:T(1024)S(1)}, ...), branch_computations={%region_7.7_spmd, %region_8.10_spmd} | conditional | flops 341445376 | bytes 16530026 | solution.py:190
  106.3 2.7 fusion.39
  109.0 2.0 copy.140
  111.0 2.2 select_reduce_fusion.1
  113.7 2.6 fusion.33
  119.5 5.2 %all_gather.37 = bf16[256,64]{1,0:T(8,128)(2,1)S(1)} all-gather(bf16[64,64]{1,0:T(8,128)(2,1)S(1)} %copy.164), channel_id=1, replica_groups=mesh['section'=2,'tok'=4,'mdl'=4] {'mdl'}, dimensions={0}, use_global_device_ids=true | all-gather | bytes 40960 | tf_op jit(solution)/shard_map/all_gather | solution.py:133
  124.7 15.6 %all_gather.38 = bf16[1024,64]{1,0:T(8,128)(2,1)S(1)} all-gather(bf16[256,64]{1,0:T(8,128)(2,1)S(1)} %all_gather.37), channel_id=1, replica_groups=mesh['section'=2,'tok'=4,'mdl'=4] {'tok'}, dimensions={0}, use_global_device_ids=true | all-gather | bytes 163840 | tf_op jit(solution)/shard_map/all_gather | solution.py:142
  140.5 3.0 copy.166
  144.4 24.0 %while.31 = (s32[]{:T(128)}, f32[256,4]{0,1:T(4,128)S(1)}, f32[256,4]{0,1:T(4,128)S(1)}, f32[256,4,128]{2,0,1:T(8,128)}, pred[]{:T(512)}, /*index=5*/s32[1024]{0...) while((s32[]{:T(128)}, f32[256,4]{0,1:T(4,128)S(1)}, ...), condition=%wide.region_35.36_spmd.clone, body=%wide.region_30.35_spmd.clone.sunk | while | flops 341445376 | bytes 18104192 | solution.py:192
  144.4 12.0 %conditional.19 = ((f32[256,4]{0,1:T(4,128)S(1)}, f32[256,4]{0,1:T(4,128)S(1)}, f32[256,4,128]{2,0,1:T(8,128)})) conditional(s32[]{:T(128)} %convert_element_type.425, (f32[256,4]{0,1:T(4,128)S(1)}, f32[256,4]{0,1:T(4,128)S(1)}, f32[256,4,128]{2,0,1:T(8,128)}) %tuple.183, (s32[2]{0:T(128)S(1)}, s32[]{:T(128)}, s32[1024]{0:T(1024)S(1)}, ...), branch_computations={%region_31.31_spmd, %region_32.34_spmd} | conditional | flops 341445376 | bytes 18102918 | solution.py:190
  147.3 1.8 fusion.96
  149.1 2.0 copy.144
  151.1 2.3 select_reduce_fusion.3
  153.8 2.6 fusion.90
  156.4 12.0 %conditional.19 = ((f32[256,4]{0,1:T(4,128)S(1)}, f32[256,4]{0,1:T(4,128)S(1)}, f32[256,4,128]{2,0,1:T(8,128)})) conditional(s32[]{:T(128)} %convert_element_type.425, (f32[256,4]{0,1:T(4,128)S(1)}, f32[256,4]{0,1:T(4,128)S(1)}, f32[256,4,128]{2,0,1:T(8,128)}) %tuple.183, (s32[2]{0:T(128)S(1)}, s32[]{:T(128)}, s32[1024]{0:T(1024)S(1)}, ...), branch_computations={%region_31.31_spmd, %region_32.34_spmd} | conditional | flops 341445376 | bytes 18102918 | solution.py:190
  159.3 1.8 fusion.96
  161.0 2.0 copy.144
  163.0 2.3 select_reduce_fusion.3
  165.7 2.6 fusion.90
  169.7 1.7 convolution_convert_fusion.3
  177.8 16.1 %reduce-scatter.9.cloned.1.call-done = bf16[64,2048]{1,0:T(8,128)(2,1)} async-done(((bf16[256,2048]{1,0:T(8,128)(2,1)}), bf16[64,2048]{1,0:T(8,128)(2,1)}) %reduce-scatter.9.cloned.1.call-update) | async-done | bytes 262160 | tf_op jit(solution)/shard_map/reduce_scatter | solution.py:204
  195.0 3.4 collective-permute-start.2
  198.6 5.3 %collective-permute-done.2 = bf16[64,2048]{1,0:T(8,128)(2,1)S(1)} collective-permute-done((bf16[64,2048]{1,0:T(8,128)(2,1)S(1)}, bf16[64,2048]{1,0:T(8,128)(2,1)S(1)}, u32[]{:S(2)}, u32[]{:S(2)}) %collective-permute-start.2) | collective-permute-done | bytes 262176 | tf_op jit(solution)/shard_map/ppermute | solution.py:21
  204.4 2.2 convolution_convert_fusion.1
  206.6 4.1 reshape.510
  210.7 4.8 all-to-all-start
  215.6 2.3 convolution_convert_fusion
  217.9 4.1 reshape.517
  222.0 43.8 %all-to-all-done = bf16[16,36,2048]{2,1,0:T(8,128)(2,1)} async-done(((bf16[16,36,2048]{2,1,0:T(8,128)(2,1)}), bf16[16,36,2048]{2,1,0:T(8,128)(2,1)}, u32[]{:S(2)}, u32[]{:S(2)}) %all-to-all-start) | async-done | bytes 2359328 | tf_op jit(solution)/shard_map/all_to_all | solution.py:249
  265.7 13.4 %all-to-all-start.2 = ((bf16[16,36,2048]{2,1,0:T(8,128)(2,1)}), bf16[16,36,2048]{2,1,0:T(8,128)(2,1)}, u32[]{:S(2)}, u32[]{:S(2)}) async-start(bf16[16,36,2048]{2,1,0:T(8,128)(2,1)} %reshape.517), calls=%async_computation.6 | async-start | bytes 5242880 | tf_op jit(solution)/shard_map/all_to_all | solution.py:249
  279.1 1.9 conditional.10
  281.0 4.1 reshape_transpose_reshape.10
  285.1 44.3 %all-to-all-done.2 = bf16[16,36,2048]{2,1,0:T(8,128)(2,1)} async-done(((bf16[16,36,2048]{2,1,0:T(8,128)(2,1)}), bf16[16,36,2048]{2,1,0:T(8,128)(2,1)}, u32[]{:S(2)}, u32[]{:S(2)}) %all-to-all-start.2) | async-done | bytes 2359328 | tf_op jit(solution)/shard_map/all_to_all | solution.py:249
  329.4 13.4 %all-to-all-start.1 = ((bf16[16,36,2048]{2,1,0:T(8,128)(2,1)}), bf16[16,36,2048]{2,1,0:T(8,128)(2,1)}, u32[]{:S(2)}, u32[]{:S(2)}) async-start(bf16[16,36,2048]{2,1,0:T(8,128)(2,1)} %reshape_transpose_reshape.10), calls=%async_computation.3 | async-start | bytes 5242880 | tf_op jit(solution)/shard_map/all_to_all | solution.py:278
  345.7 4.1 reshape_transpose_reshape.11
  349.7 43.5 %all-to-all-done.1 = bf16[16,36,2048]{2,1,0:T(8,128)(2,1)} async-done(((bf16[16,36,2048]{2,1,0:T(8,128)(2,1)}), bf16[16,36,2048]{2,1,0:T(8,128)(2,1)}, u32[]{:S(2)}, u32[]{:S(2)}) %all-to-all-start.1) | async-done | bytes 2359328 | tf_op jit(solution)/shard_map/all_to_all | solution.py:278
  393.2 13.4 %all-to-all-start.3 = ((bf16[16,36,2048]{2,1,0:T(8,128)(2,1)}), bf16[16,36,2048]{2,1,0:T(8,128)(2,1)}, u32[]{:S(2)}, u32[]{:S(2)}) async-start(bf16[16,36,2048]{2,1,0:T(8,128)(2,1)} %reshape_transpose_reshape.11), calls=%async_computation.7 | async-start | bytes 5242880 | tf_op jit(solution)/shard_map/all_to_all | solution.py:278
  412.2 4.1 reshape.511
  416.3 28.7 %reduce-scatter.7.cloned.1.call-done = bf16[64,2048]{1,0:T(8,128)(2,1)} async-done(((bf16[256,2048]{1,0:T(8,128)(2,1)}), bf16[64,2048]{1,0:T(8,128)(2,1)}) %reduce-scatter.7.cloned.1.call-update) | async-done | bytes 262160 | tf_op jit(solution)/shard_map/reduce_scatter | solution.py:225
  445.0 3.8 fusion.136
  450.2 6.8 %all-to-all-done.3 = bf16[16,36,2048]{2,1,0:T(8,128)(2,1)} async-done(((bf16[16,36,2048]{2,1,0:T(8,128)(2,1)}), bf16[16,36,2048]{2,1,0:T(8,128)(2,1)}, u32[]{:S(2)}, u32[]{:S(2)}) %all-to-all-start.3) | async-done | bytes 2359328 | tf_op jit(solution)/shard_map/all_to_all | solution.py:278
  457.0 4.3 reshape.518
  461.3 3.1 fusion.161
  464.4 11.4 %reduce-scatter.11.cloned.1.call-done = bf16[64,2048]{1,0:T(8,128)(2,1)} async-done(((bf16[256,2048]{1,0:T(8,128)(2,1)}), bf16[64,2048]{1,0:T(8,128)(2,1)}) %reduce-scatter.11.cloned.1.call-update) | async-done | bytes 262160 | tf_op jit(solution)/shard_map/reduce_scatter | solution.py:225
  475.8 1.8 fusion.135
  (240 shorter events, 57.6 us)
Async XLA Ops:
  6.5 111.1 %copy-start = (bf16[512,2048]{1,0:T(8,128)(2,1)S(1)}, bf16[512,2048]{1,0:T(8,128)(2,1)}, u32[]{:S(2)}) copy-start(bf16[512,2048]{1,0:T(8,128)(2,1)} %param.46) | copy-start | bytes 6291460
  6.5 79.9 %all-gather.5.cloned.1.call-start = ((), (), s32[]{:S(2)}) async-start(), calls=%async_computation.8 | async-start | bytes 2621440 | tf_op jit(solution)/shard_map/all_gather | solution.py:141
  8.0 3.2 copy-start.12
  8.0 3.2 copy-start.14
  8.0 3.2 copy-start.17
  11.2 23.3 %copy-start.8 = (bf16[512,1024]{1,0:T(8,128)(2,1)S(1)}, bf16[512,1024]{1,0:T(8,128)(2,1)}, u32[]{:S(2)}) copy-start(bf16[512,1024]{1,0:T(8,128)(2,1)} %param.45) | copy-start | bytes 3145732
  11.3 3.2 copy-start.5
  27.0 8.9 %copy-start.11 = (s32[1,1024]{1,0:T(1,128)S(1)}, s32[1,1024]{1,0:T(1,128)}, u32[]{:S(2)}) copy-start(s32[1,1024]{1,0:T(1,128)} %get-tuple-element.979) | copy-start | bytes 12292
  27.0 8.9 %copy-start.15 = (f32[2048]{0:T(1024)S(1)}, f32[2048]{0:T(1024)}, u32[]{:S(2)}) copy-start(f32[2048]{0:T(1024)} %param.41) | copy-start | bytes 24580
  27.0 9.0 %copy-start.18 = (f32[512]{0:T(512)S(1)}, f32[512]{0:T(512)}, u32[]{:S(2)}) copy-start(f32[512]{0:T(512)} %param.44) | copy-start | bytes 6148
  35.9 104.6 %all-gather.9.cloned.1.call-start = ((), (), s32[]{:S(2)}) async-start(), calls=%async_computation.12 | async-start | bytes 2621440 | tf_op jit(solution)/shard_map/all_gather | solution.py:141
  36.0 3.2 copy-start.6
  41.0 4.9 %copy-start.4 = (bf16[1,256,2048]{2,1,0:T(8,128)(2,1)S(1)}, bf16[1,256,2048]{2,1,0:T(8,128)(2,1)}, u32[]{:S(2)}) copy-start(bf16[1,256,2048]{2,1,0:T(8,128)(2,1)} %get-tuple-element.534) | copy-start | bytes 3145732 | tf_op jit(solution)/shard_map/cond
  49.5 31.6 %copy-start.2 = (bf16[256,4,192]{2,0,1:T(8,128)(2,1)}, bf16[256,4,192]{2,0,1:T(8,128)(2,1)S(1)}, u32[]{:S(2)}) copy-start(bf16[256,4,192]{2,0,1:T(8,128)(2,1)S(1)} %get-tuple-element.1159) | copy-start | bytes 1179652
  55.4 25.7 %copy-start.13 = (s32[1,1024]{1,0:T(1,128)S(1)}, s32[1,1024]{1,0:T(1,128)}, u32[]{:S(2)}) copy-start(s32[1,1024]{1,0:T(1,128)} %copy-done.12) | copy-start | bytes 12292
  58.0 117.4 %reduce-scatter.5.cloned.1.call-start = ((), (), s32[]{:S(2)}) async-start(), calls=%async_computation.9 | async-start | bytes 1310720 | tf_op jit(solution)/shard_map/reduce_scatter | solution.py:204
  119.3 74.6 %reduce-scatter.9.cloned.1.call-start = ((), (), s32[]{:S(2)}) async-start(), calls=%async_computation.13 | async-start | bytes 1310720 | tf_op jit(solution)/shard_map/reduce_scatter | solution.py:204
  145.6 1.6 copy-start.3
  157.6 1.6 copy-start.3
  169.7 1.8 copy-start.19
  171.4 32.7 %copy-start.16 = (f32[2048]{0:T(1024)S(1)}, f32[2048]{0:T(1024)}, u32[]{:S(2)}) copy-start(f32[2048]{0:T(1024)} %param.47) | copy-start | bytes 24580
  176.5 21.9 %collective-permute-start = (bf16[64,2048]{1,0:T(8,128)(2,1)S(1)}, bf16[64,2048]{1,0:T(8,128)(2,1)S(1)}, u32[]{:S(2)}, u32[]{:S(2)}) collective-permute-start(bf16[64,2048]{1,0:T(8,128)(2,1)S(1)} %fusion.133), channel_id=1, source_target_pairs={{0,16},{1,17},{2,18},{3,19},{4,20},{5,21},{6,22},{7,23},{8,24},{9,... | collective-permute-start | bytes 786440 | tf_op jit(solution)/shard_map/ppermute | solution.py:21
  195.0 8.9 %collective-permute-start.2 = (bf16[64,2048]{1,0:T(8,128)(2,1)S(1)}, bf16[64,2048]{1,0:T(8,128)(2,1)S(1)}, u32[]{:S(2)}, u32[]{:S(2)}) collective-permute-start(bf16[64,2048]{1,0:T(8,128)(2,1)S(1)} %fusion.132), channel_id=1, source_target_pairs={{0,16},{1,17},{2,18},{3,19},{4,20},{5,21},{6,22},{7,23},{8,24},{9,... | collective-permute-start | bytes 786440 | tf_op jit(solution)/shard_map/ppermute | solution.py:21
  204.3 6.3 %copy-start.10 = (bf16[64,2048]{1,0:T(8,128)(2,1)}, bf16[64,2048]{1,0:T(8,128)(2,1)S(1)}, u32[]{:S(2)}) copy-start(bf16[64,2048]{1,0:T(8,128)(2,1)S(1)} %get-tuple-element.978) | copy-start | bytes 786436
  204.3 11.3 %copy-start.9 = (bf16[64,2048]{1,0:T(8,128)(2,1)}, bf16[64,2048]{1,0:T(8,128)(2,1)S(1)}, u32[]{:S(2)}) copy-start(bf16[64,2048]{1,0:T(8,128)(2,1)S(1)} %get-tuple-element.977) | copy-start | bytes 786436
  210.7 55.1 %all-to-all-start = ((bf16[16,36,2048]{2,1,0:T(8,128)(2,1)}), bf16[16,36,2048]{2,1,0:T(8,128)(2,1)}, u32[]{:S(2)}, u32[]{:S(2)}) async-start(bf16[16,36,2048]{2,1,0:T(8,128)(2,1)} %reshape.510), calls=%async_computation.2 | async-start | bytes 5242880 | tf_op jit(solution)/shard_map/all_to_all | solution.py:249
  265.7 63.7 %all-to-all-start.2 = ((bf16[16,36,2048]{2,1,0:T(8,128)(2,1)}), bf16[16,36,2048]{2,1,0:T(8,128)(2,1)}, u32[]{:S(2)}, u32[]{:S(2)}) async-start(bf16[16,36,2048]{2,1,0:T(8,128)(2,1)} %reshape.517), calls=%async_computation.6 | async-start | bytes 5242880 | tf_op jit(solution)/shard_map/all_to_all | solution.py:249
  329.4 63.8 %all-to-all-start.1 = ((bf16[16,36,2048]{2,1,0:T(8,128)(2,1)}), bf16[16,36,2048]{2,1,0:T(8,128)(2,1)}, u32[]{:S(2)}, u32[]{:S(2)}) async-start(bf16[16,36,2048]{2,1,0:T(8,128)(2,1)} %reshape_transpose_reshape.10), calls=%async_computation.3 | async-start | bytes 5242880 | tf_op jit(solution)/shard_map/all_to_all | solution.py:278
  342.8 63.9 %all-gather.7.cloned.1.call-start = ((), (), s32[]{:S(2)}) async-start(), calls=%async_computation.10 | async-start | bytes 1310720 | tf_op jit(solution)/shard_map/all_gather | solution.py:214
  343.4 66.6 %all-gather.11.cloned.1.call-start = ((), (), s32[]{:S(2)}) async-start(), calls=%async_computation.14 | async-start | bytes 1310720 | tf_op jit(solution)/shard_map/all_gather | solution.py:214
  393.2 63.7 %all-to-all-start.3 = ((bf16[16,36,2048]{2,1,0:T(8,128)(2,1)}), bf16[16,36,2048]{2,1,0:T(8,128)(2,1)}, u32[]{:S(2)}, u32[]{:S(2)}) async-start(bf16[16,36,2048]{2,1,0:T(8,128)(2,1)} %reshape_transpose_reshape.11), calls=%async_computation.7 | async-start | bytes 5242880 | tf_op jit(solution)/shard_map/all_to_all | solution.py:278
  406.6 38.5 %reduce-scatter.7.cloned.1.call-start = ((), (), s32[]{:S(2)}) async-start(), calls=%async_computation.11 | async-start | bytes 1310720 | tf_op jit(solution)/shard_map/reduce_scatter | solution.py:225
  406.7 1.6 copy-start.7
  409.9 65.8 %reduce-scatter.11.cloned.1.call-start = ((), (), s32[]{:S(2)}) async-start(), calls=%async_computation.15 | async-start | bytes 1310720 | tf_op jit(solution)/shard_map/reduce_scatter | solution.py:225
  410.1 1.7 copy-start.20
  448.9 26.9 %collective-permute-start.1 = (bf16[1,64,2048]{2,1,0:T(8,128)(2,1)}, bf16[1,64,2048]{2,1,0:T(8,128)(2,1)S(1)}, u32[]{:S(2)}, u32[]{:S(2)}) collective-permute-start(bf16[1,64,2048]{2,1,0:T(8,128)(2,1)} %fusion.136), channel_id=1, source_target_pairs={{16,0},{17,1},{18,2},{19,3},{20,4},{21,5},{22,6},{23,7},{24,8},{25... | collective-permute-start | bytes 786440 | tf_op jit(solution)/shard_map/ppermute | solution.py:21
  457.0 20.6 %copy-start.1 = (bf16[512,2048]{1,0:T(8,128)(2,1)S(1)}, bf16[512,2048]{1,0:T(8,128)(2,1)}, u32[]{:S(2)}) copy-start(bf16[512,2048]{1,0:T(8,128)(2,1)} %param.46) | copy-start | bytes 6291460
Sparse Core Ops, SparseCore 0:
  36.0 50.3 all-gather.4
  88.0 45.1 all-gather.8
  135.8 26.3 reduce-scatter.4
  171.6 22.3 reduce-scatter.8
  344.9 27.5 all-gather.6
  373.9 22.9 all-gather.10
  410.1 34.9 reduce-scatter.6
  447.7 28.0 reduce-scatter.10
where the time goes:
time: 493 us; the launch traced here: 485 us
  waiting for transfers between devices  206 us (42%)
  local copies, waits for them, and re-layouts  76.7 us (16%)
  matrix products  56.7 us (12%)
  blocking collectives  56.4 us (11%)
  starting transfers between devices  51.1 us (10%)
  other arithmetic  19.5 us (4%)
  between operations  14.5 us (3%)
    all_to_all x2, waiting for transfers between devices, shards(): lax.all_to_all(outgoing, ('tok', 'mdl'), split_axis=0, concat_axis=0, til...  88 us
    all_to_all x2, waiting for transfers between devices, shards(): lax.all_to_all(processed, ('tok', 'mdl'), split_axis=0, concat_axis=0, ti...  50.3 us
    reduce_scatter x2, waiting for transfers between devices, shards(): lax.psum_scatter(jnp.dot(shared_act, w_shared_down, preferred_element_typ...  40.1 us
    all_gather x2, blocking collectives, shards(): rope_keys = lax.all_gather(rope_rows, 'tok', axis=0, tiled=True)  32.5 us
    all_to_all x2, starting transfers between devices, shards(): lax.all_to_all(processed, ('tok', 'mdl'), split_axis=0, concat_axis=0, ti...  26.7 us
    another operation x18, local copies, waits for them, and re-layouts  23.1 us
    all_to_all x2, starting transfers between devices, shards(): lax.all_to_all(outgoing, ('tok', 'mdl'), split_axis=0, concat_axis=0, til...  18.1 us
    reduce_scatter x2, waiting for transfers between devices, shards(): lax.psum_scatter(jnp.dot(attended, w_out, preferred_element_type=jnp.floa...  16.1 us
  transfers between devices with their start and end apart: 15, of which 9 were waited for; matrix products, arithmetic and copies ran while one was open for 25% of the time, Pallas kernels for 0%

commit v1 on v0

v1 whole, which is shorter than its diff:
```python
import functools
import math

import jax
import jax.numpy as jnp
from jax import lax
from jax.experimental import pallas as pl
from jax.experimental.pallas import tpu as pltpu
from jax.sharding import PartitionSpec as P

NOPE = 128
ROPE = 64
VDIM = 128
LATENT = 512
SEGS = 4
EPS = 1e-06
BF16 = jnp.bfloat16
F32 = jnp.float32


def rms_scale(values, gain_vec):
    values = values.astype(F32)
    return values * lax.rsqrt(jnp.mean(values * values, axis=-1, keepdims=True) + EPS) * gain_vec


def rotary_tables(positions):
    half_width = ROPE // 2
    frequency = 10000.0 ** (-jnp.arange(half_width, dtype=F32) / half_width)
    angles = positions.astype(F32)[:, None] * frequency[None, :]
    cosine = jnp.cos(angles)
    sine = jnp.sin(angles)
    return jnp.concatenate([cosine, cosine], axis=1), jnp.concatenate([-sine, sine], axis=1)


def turned(values, cosine, sine):
    half_width = values.shape[-1] // 2
    swapped = jnp.concatenate([values[:, half_width:], values[:, :half_width]], axis=1)
    return values * cosine + swapped * sine


def silu_mul(gate, up):
    return gate / (1.0 + jnp.exp(-gate)) * up


def attend_kernel(
    q_ref, lat_ref, kr_ref, wkv_ref, wo_ref, cos_ref, sin_ref, low_ref, high_ref, out_ref, att_ref
):
    heads = wo_ref.shape[0] // VDIM
    width = NOPE + ROPE
    span = lat_ref.shape[0]
    scale = 1.0 / math.sqrt(width)
    rope_keys = kr_ref[...]
    cosine, sine = cos_ref[...], sin_ref[...]
    key_index = lax.broadcasted_iota(jnp.int32, (q_ref.shape[0], span), 1)
    allowed = (key_index >= low_ref[...]) & (key_index <= high_ref[...])
    contract = (((1,), (1,)), ((), ()))
    for h in range(heads):
        kv = jnp.dot(
            lat_ref[...],
            wkv_ref[:, h * (NOPE + VDIM) : (h + 1) * (NOPE + VDIM)],
            preferred_element_type=F32,
        ).astype(BF16)
        q_nope = q_ref[:, h * width : h * width + NOPE].astype(BF16)
        q_rope = turned(q_ref[:, h * width + NOPE : (h + 1) * width], cosine, sine).astype(BF16)
        scores = lax.dot_general(q_nope, kv[:, :NOPE], contract, preferred_element_type=F32)
        scores += lax.dot_general(q_rope, rope_keys, contract, preferred_element_type=F32)
        scores = jnp.where(allowed, scores * scale, -1e30)
        top = jnp.max(scores, axis=1, keepdims=True)
        weights = jnp.where(allowed, jnp.exp(scores - top), 0.0)
        total = jnp.sum(weights, axis=1, keepdims=True)
        summed = jnp.dot(weights.astype(BF16), kv[:, NOPE:], preferred_element_type=F32)
        att_ref[:, h * VDIM : (h + 1) * VDIM] = (summed / total).astype(BF16)
    out_ref[...] = jnp.dot(att_ref[...], wo_ref[...], preferred_element_type=F32).astype(BF16)


def attend(queries, latent, rope_keys, w_kv_up, w_out, cosine, sine, low, high):
    rows = queries.shape[0]
    return pl.pallas_call(
        attend_kernel,
        out_shape=jax.ShapeDtypeStruct((rows, w_out.shape[1]), BF16),
        in_specs=[pl.BlockSpec(memory_space=pltpu.VMEM)] * 9,
        out_specs=pl.BlockSpec(memory_space=pltpu.VMEM),
        scratch_shapes=[pltpu.VMEM((rows, w_out.shape[0]), BF16)],
        compiler_params=pltpu.CompilerParams(vmem_limit_bytes=40 * 2**20),
        cost_estimate=pl.CostEstimate(
            flops=3 * 10**9, bytes_accessed=6 * 10**6, transcendentals=10**6
        ),
    )(queries, latent, rope_keys, w_kv_up, w_out, cosine, sine, low, high)


def shards(
    layer_input,
    segment_ids,
    route_ids,
    route_weights,
    attn_gain,
    w_query,
    w_kv_down,
    latent_gain,
    w_kv_up,
    w_out,
    ffn_gain,
    w_shared_gate,
    w_shared_up,
    w_shared_down,
    w_expert_gate,
    w_expert_up,
    w_expert_down,
):
    n_mdl = lax.axis_size("mdl")
    n_wide = lax.axis_size(("tok", "mdl"))
    section_id = lax.axis_index("section")
    tok_rank = lax.axis_index("tok")
    mdl_rank = lax.axis_index("mdl")
    micro_count, tok_dev, model_width = layer_input.shape
    per_section = micro_count // lax.axis_size("section")
    row_dev = tok_dev // n_mdl
    pack = segment_ids.shape[1]
    expert_dev = w_expert_gate.shape[0]
    expert_total = expert_dev * n_wide
    span = min(pack, pack // 2 + tok_dev)
    results = []
    for step in range(per_section):
        batch = section_id * per_section + step
        rows_in = lax.dynamic_index_in_dim(layer_input, batch, 0, keepdims=False)
        segment_row = lax.dynamic_index_in_dim(segment_ids, batch, 0, keepdims=False)
        chosen = lax.dynamic_index_in_dim(route_ids, batch, 0, keepdims=False)
        chosen_weights = lax.dynamic_index_in_dim(route_weights, batch, 0, keepdims=False)
        labels = jnp.arange(expert_total, dtype=jnp.int32)
        combining = jnp.sum(
            jnp.where(chosen[:, :, None] == labels, chosen_weights[:, :, None], 0.0), axis=1
        )
        all_combining = lax.all_gather(combining, ("tok", "mdl"), axis=0, tiled=True)

        query_start = tok_rank * tok_dev
        query_seg = lax.dynamic_slice_in_dim(segment_row, query_start, tok_dev)
        firsts = jnp.sum((segment_row[None, :] < query_seg[:, None]).astype(jnp.int32), axis=1)
        query_index = query_start + jnp.arange(tok_dev, dtype=jnp.int32)
        cosine, sine = rotary_tables(query_index - firsts)
        window = jnp.clip(query_start - pack // 2, 0, pack - span)
        low = (firsts - window)[:, None]
        high = (query_index - window)[:, None]

        own = mdl_rank * row_dev
        normed = rms_scale(rows_in, attn_gain).astype(BF16)
        own_normed = lax.dynamic_slice_in_dim(normed, own, row_dev)
        compressed = jnp.dot(own_normed, w_kv_down, preferred_element_type=F32)
        latent = rms_scale(compressed[:, :LATENT], latent_gain).astype(BF16)
        key_rope = turned(
            compressed[:, LATENT:],
            lax.dynamic_slice_in_dim(cosine, own, row_dev),
            lax.dynamic_slice_in_dim(sine, own, row_dev),
        ).astype(BF16)
        keys = lax.all_gather(
            jnp.concatenate([latent, key_rope], axis=1), ("tok", "mdl"), axis=0, tiled=True
        )
        queries = jnp.dot(normed, w_query, preferred_element_type=F32)
        keys = lax.dynamic_slice_in_dim(keys, window, span)
        partial = attend(
            queries, keys[:, :LATENT], keys[:, LATENT:], w_kv_up, w_out, cosine, sine, low, high
        )
        mixed = lax.psum_scatter(partial, "mdl", scatter_dimension=0, tiled=True)
        own_input = lax.dynamic_slice_in_dim(rows_in, own, row_dev)
        residual = (own_input.astype(F32) + mixed.astype(F32)).astype(BF16)
        normed_ffn = rms_scale(residual, ffn_gain).astype(BF16)
        all_rows = lax.all_gather(normed_ffn, ("tok", "mdl"), axis=0, tiled=True)

        group_rows = lax.dynamic_slice_in_dim(all_rows, query_start, tok_dev)
        shared_act = silu_mul(
            jnp.dot(group_rows, w_shared_gate, preferred_element_type=F32),
            jnp.dot(group_rows, w_shared_up, preferred_element_type=F32),
        ).astype(BF16)
        shared_part = jnp.dot(shared_act, w_shared_down, preferred_element_type=F32)
        outgoing = jnp.zeros((pack, model_width), F32)
        for local in range(expert_dev):
            expert = (tok_rank * n_mdl + mdl_rank) * expert_dev + local
            row_weight = lax.dynamic_slice_in_dim(all_combining, expert, 1, axis=1)
            act = silu_mul(
                jnp.dot(all_rows, w_expert_gate[local], preferred_element_type=F32),
                jnp.dot(all_rows, w_expert_up[local], preferred_element_type=F32),
            )
            act = (act * row_weight).astype(BF16)
            outgoing += jnp.dot(act, w_expert_down[local], preferred_element_type=F32)
        group_sum = lax.dynamic_slice_in_dim(outgoing, query_start, tok_dev) + shared_part
        outgoing = lax.dynamic_update_slice_in_dim(outgoing, group_sum, query_start, 0)
        summed = lax.psum_scatter(
            outgoing.astype(BF16), ("tok", "mdl"), scatter_dimension=0, tiled=True
        )
        results.append((residual.astype(F32) + summed.astype(F32)).astype(BF16))
    return jnp.stack(results)


def solution(mesh):
    in_specs = (
        P(None, "tok", None),
        P(),
        P(None, ("tok", "mdl"), None),
        P(None, ("tok", "mdl"), None),
        P(),
        P(None, "mdl"),
        P(),
        P(),
        P(None, "mdl"),
        P("mdl", None),
        P(),
        P(None, "mdl"),
        P(None, "mdl"),
        P("mdl", None),
        P(("tok", "mdl"), None, None),
        P(("tok", "mdl"), None, None),
        P(("tok", "mdl"), None, None),
    )
    out_specs = P("section", ("tok", "mdl"), None)
    return jax.shard_map(shards, mesh=mesh, in_specs=in_specs, out_specs=out_specs, check_vma=False)
```

time: 493 us -> 263 us (0.53); the launches traced: 485 us -> 262 us
  local copies, waits for them, and re-layouts: 76.7 us -> 12.2 us
  starting transfers between devices: 51.1 us -> 0.13 us
  waiting for transfers between devices: 206 us -> 158 us
  blocking collectives: 56.4 us -> 21.2 us
  matrix products: 56.7 us -> 36.4 us
    all_to_all x4 -> x0, waiting for transfers between devices: 138 us -> none  [the longest x2 88 us: shards(): lax.all_to_all(outgoing, ('tok', 'mdl'), split_axis=0, concat_axis=0, til...]
    all_gather x4 -> x2, waiting for transfers between devices: 5.31 us -> 62.9 us  [the longest x1 35.5 us: shards(): lax.all_gather(jnp.concatenate([latent, key_rope], axis=1), ('tok', 'mdl'...]
    all_to_all x4 -> x0, starting transfers between devices: 44.9 us -> none  [the longest x2 26.7 us: shards(): lax.all_to_all(processed, ('tok', 'mdl'), split_axis=0, concat_axis=0, ti...]
    reduce_scatter x4 -> x2, waiting for transfers between devices: 56.2 us -> 94.8 us  [the longest x1 71 us: shards(): lax.psum_scatter(outgoing.astype(BF16), ('tok', 'mdl'), scatter_dimension...]
    all_gather x6 -> x1, blocking collectives: 56.4 us -> 21.2 us  [shards(): lax.all_gather(combining, ('tok', 'mdl'), axis=0, tiled=True)]
    another operation x20 -> x0, local copies, waits for them, and re-layouts: 31.3 us -> none
    dot_general x26 -> x6, matrix products: 56.7 us -> 36.4 us  [the longest x1 13 us: shards(): outgoing += jnp.dot(act, w_expert_down[local], preferred_element_type=F32)]
    reshape x6 -> x0, local copies, waits for them, and re-layouts: 18.3 us -> none  [the longest x2 8.45 us: shards(): returned.reshape(slot_total, model_width).astype(jnp.float32)]
  transfers between devices with their start and end apart: 15 -> 4, of which waited for: 9 -> 4; matrix products, arithmetic and copies ran while one was open for 25% -> 3% of each run, Pallas kernels for 0% -> 0%
where the time goes in v1:
time: 263 us; the launch traced here: 262 us
  waiting for transfers between devices  158 us (60%)
  matrix products  36.4 us (14%)
  blocking collectives  21.2 us (8%)
  other arithmetic  16.7 us (6%)
  between operations  13.4 us (5%)
  local copies, waits for them, and re-layouts  12.2 us (5%)
  Pallas kernels  4.63 us (2%)
    reduce_scatter x1, waiting for transfers between devices, shards(): lax.psum_scatter(outgoing.astype(BF16), ('tok', 'mdl'), scatter_dimension...  71 us
    all_gather x1, waiting for transfers between devices, shards(): lax.all_gather(jnp.concatenate([latent, key_rope], axis=1), ('tok', 'mdl'...  35.5 us
    all_gather x1, waiting for transfers between devices, shards(): all_rows = lax.all_gather(normed_ffn, ('tok', 'mdl'), axis=0, tiled=True)  27.4 us
    reduce_scatter x1, waiting for transfers between devices, shards(): mixed = lax.psum_scatter(partial, 'mdl', scatter_dimension=0, tiled=True)  23.8 us
    all_gather x1, blocking collectives, shards(): lax.all_gather(combining, ('tok', 'mdl'), axis=0, tiled=True)  21.2 us
    dot_general x1, matrix products, shards(): outgoing += jnp.dot(act, w_expert_down[local], preferred_element_type=F32)  13 us
    unnamed x33, local copies, waits for them, and re-layouts  8 us
    dot_general x1, matrix products, shards(): jnp.dot(all_rows, w_expert_up[local], preferred_element_type=F32)  7.26 us
  transfers between devices with their start and end apart: 4, of which 4 were waited for; matrix products, arithmetic and copies ran while one was open for 3% of the time, Pallas kernels for 0%

profile of v1, /device:TPU:0, one launch (start us, length us, event | category | flops | bytes accessed | tf_op | source)
XLA Modules:
  0.0 262.4 jit_solution(17605259840490792161)
XLA Ops:
  6.5 0.0 copy-start
  6.5 0.0 all-gather.4.cloned.1.call-start
  6.6 0.0 copy-start.12
  6.6 1.7 fusion.9
  8.2 1.6 fusion.11
  9.8 0.0 copy-start.6
  9.8 0.9 copy-done.6
  10.8 2.5 fusion.30
  13.2 0.1 multiply_reduce_fusion
  13.3 0.1 fusion.46
  13.4 0.0 copy-done.11
  13.5 0.1 dynamic_slice.47
  13.6 0.2 convert_reduce_fusion
  13.8 0.5 multiply_cosine_fusion
  14.4 0.0 copy-done.12
  14.4 0.0 copy-start.7
  14.4 0.0 copy-start.8
  14.4 0.0 copy-start.9
  14.4 0.1 multiply_convert_fusion.1
  14.5 0.1 fusion.36
  14.6 0.4 copy-done.7
  15.0 0.0 copy-done.8
  15.1 0.0 copy-done.9
  15.1 0.6 pad_maximum_fusion.2
  15.7 0.0 all-gather.4.cloned.1.call-update
  15.8 0.0 reduce-scatter.3.cloned.1.call-start
  15.8 0.1 copy.39.low_ref
  15.9 0.7 add_subtract_fusion.high_ref
  16.6 1.2 pad_maximum_fusion
  17.8 4.1 %fusion.47.q_ref = f32[256,768]{1,0:T(8,128)} fusion(bf16[256,2048]{1,0:T(8,128)(2,1)} %copy-done.6, bf16[2048,768]{1,0:T(8,128)(2,1)} %param.22), kind=kOutput, calls=%fused_computation.77 | convolution fusion | flops 805306368 | bytes 4980736 | tf_op jit(solution)/shard_map/dot_general | solution.py:157
  21.9 35.5 %all-gather.4.cloned.1.call-done = bf16[1024,576]{1,0:T(8,128)(2,1)} async-done(((bf16[64,576]{1,0:T(8,128)(2,1)}), bf16[1024,576]{1,0:T(8,128)(2,1)}) %all-gather.4.cloned.1.call-update) | async-done | bytes 1179664 | tf_op jit(solution)/shard_map/all_gather | solution.py:154
  57.4 1.3 constant_dynamic-slice_fusion.lat_ref
  58.7 1.1 dynamic-slice.4.kr_ref
  59.8 0.0 copy-start.2
  59.8 0.9 copy-done.2
  60.7 1.6 copy-done.3
  62.3 1.2 copy-done.4
  63.5 1.1 copy-done.5
  64.7 4.6 %shard_map.163 = bf16[256,2048]{1,0:T(8,128)(2,1)S(1)} custom-call(f32[256,768]{1,0:T(8,128)S(1)} %copy-done.5, bf16[768,512]{1,0:T(8,128)(2,1)S(1)} %constant_dynamic-slice_fusion.lat_ref, bf16[768,64]{1,0:T(8,128)(2,1)S(1)} %dynamic-slice.4.kr_ref, bf16[512,1024]{1,0:T(8,128)(2,1)S(1)} %copy-done.4, bf16[512,2048]{1,0:T(8,128)(2,1)S(1)} %copy-done.3, ...), custom_call_target="tpu_custom_call" | custom-call | flops 3000000000 | bytes 6000000 | tf_op jit(solution)/shard_map/pallas_call | solution.py:78
  69.3 0.0 copy-start.1
  69.3 1.0 copy-done.1
  70.3 0.0 reduce-scatter.3.cloned.1.call-update
  70.3 0.0 all-gather.6.cloned.1.call-start
  70.4 23.8 %reduce-scatter.3.cloned.1.call-done = bf16[64,2048]{1,0:T(8,128)(2,1)} async-done(((bf16[256,2048]{1,0:T(8,128)(2,1)}), bf16[64,2048]{1,0:T(8,128)(2,1)}) %reduce-scatter.3.cloned.1.call-update) | async-done | bytes 262160 | tf_op jit(solution)/shard_map/reduce_scatter | solution.py:162
  94.2 1.3 fusion.19
  95.5 0.0 copy-done.10
  95.5 0.8 fusion.21
  96.3 0.0 all-gather.6.cloned.1.call-update
  96.3 0.0 reduce-scatter.5.cloned.1.call-start
  96.4 0.0 copy-done.13
  96.4 0.7 constant_dynamic-slice_fusion.2
  97.2 21.2 %all-gather = f32[16,64,16]{1,2,0:T(8,128)S(1)} all-gather(f32[1,64,16]{1,2,0:T(8,128)S(1)} %bitcast.44), channel_id=1, replica_groups=mesh['section'=2,'tok'=4,'mdl'=4] {'tok','mdl'}, dimensions={0}, use_global_device_ids=true | all-gather | bytes 69632 | tf_op jit(solution)/shard_map/all_gather | solution.py:133
  118.4 0.7 reshape.73
  119.2 0.8 constant_dynamic-slice_fusion.1
  119.9 27.4 %all-gather.6.cloned.1.call-done = bf16[1024,2048]{1,0:T(8,128)(2,1)} async-done(((bf16[64,2048]{1,0:T(8,128)(2,1)}), bf16[1024,2048]{1,0:T(8,128)(2,1)}) %all-gather.6.cloned.1.call-update) | async-done | bytes 4194320 | tf_op jit(solution)/shard_map/all_gather | solution.py:166
  147.3 3.6 %fusion.15 = f32[256,512]{1,0:T(8,128)} fusion(bf16[2048,512]{1,0:T(8,128)(2,1)} %param.28, bf16[1024,2048]{1,0:T(8,128)(2,1)} %all-gather.6.cloned.1.call-done, s32[]{:T(128)S(6)} %select_n.40), kind=kOutput, calls=%fused_computation.18 | convolution fusion | flops 536870912 | bytes 3670020 | tf_op jit(solution)/shard_map/dot_general | solution.py:170
  150.9 0.0 copy-done.14
  150.9 7.3 %fusion.2 = f32[1024,768]{1,0:T(8,128)} fusion(bf16[1024,2048]{1,0:T(8,128)(2,1)} %all-gather.6.cloned.1.call-done, bf16[1,2048,768]{2,1,0:T(8,128)(2,1)S(1)} %copy-done.14), kind=kOutput, calls=%fused_computation.2 | convolution fusion | flops 3221225472 | bytes 10485760 | tf_op jit(solution)/shard_map/dot_general | solution.py:180
  158.2 13.0 %fusion = f32[1024,2048]{1,0:T(8,128)} fusion(bf16[1,768,2048]{2,1,0:T(8,128)(2,1)S(1)} %copy-done, f32[1024,768]{1,0:T(8,128)} %fusion.2, bf16[1024,2048]{1,0:T(8,128)(2,1)} %all-gather.6.cloned.1.call-done, bf16[1,2048,768]{2,1,0:T(8,128)(2,1)} %param.31, f32[1024]{0:T(1024)S(1)} %bitcast.49), kind=kOutput, calls=%fused_computation | convolution fusion | flops 6447169536 | bytes 22024192 | tf_op jit(solution)/shard_map/dot_general | solution.py:183
  171.1 6.0 %fusion.6 = f32[1024,2048]{1,0:T(8,128)} fusion(f32[1024,2048]{1,0:T(8,128)} %fusion, s32[]{:T(128)S(6)} %select_n.40, bf16[512,2048]{1,0:T(8,128)(2,1)} %param.30, bf16[2048,512]{1,0:T(8,128)(2,1)} %param.29, bf16[1024,2048]{1,0:T(8,128)(2,1)} %all-gather.6.cloned.1.call-done, f32[256,512]{1,0:T(8,128)} %fusion.15), kind=kOutput, calls=%fused_computation.8 | convolution fusion | flops 1074921472 | bytes 9962496 | tf_op jit(solution)/shard_map/dot_general | solution.py:173
  177.1 6.0 %convert_element_type.74 = bf16[1024,2048]{1,0:T(8,128)(2,1)} convert(f32[1024,2048]{1,0:T(8,128)} %fusion.6) | non-fusion elementwise | flops 2097152 | bytes 12582912 | tf_op jit(solution)/shard_map/convert_element_type | solution.py:187
  183.1 0.0 reduce-scatter.5.cloned.1.call-update
  183.1 71.0 %reduce-scatter.5.cloned.1.call-done = bf16[64,2048]{1,0:T(8,128)(2,1)} async-done(((bf16[1024,2048]{1,0:T(8,128)(2,1)}), bf16[64,2048]{1,0:T(8,128)(2,1)}) %reduce-scatter.5.cloned.1.call-update) | async-done | bytes 262160 | tf_op jit(solution)/shard_map/reduce_scatter | solution.py:186
  254.2 1.7 fusion.28
  (19 shorter events, 0.1 us)
Async XLA Ops:
  6.5 151.6 %copy-start = (bf16[1,768,2048]{2,1,0:T(8,128)(2,1)S(1)}, bf16[1,768,2048]{2,1,0:T(8,128)(2,1)}, u32[]{:S(2)}) copy-start(bf16[1,768,2048]{2,1,0:T(8,128)(2,1)} %param.33) | copy-start | bytes 9437188
  6.5 6.9 %copy-start.11 = (s32[2,1024]{1,0:T(2,128)S(1)}, s32[2,1024]{1,0:T(2,128)}, u32[]{:S(2)}) copy-start(s32[2,1024]{1,0:T(2,128)} %param.18) | copy-start | bytes 24580
  6.5 50.9 %all-gather.4.cloned.1.call-start = ((), (), s32[]{:S(2)}) async-start(), calls=%async_computation.2 | async-start | bytes 1392640 | tf_op jit(solution)/shard_map/all_gather | solution.py:154
  6.6 7.8 %copy-start.12 = (f32[512]{0:T(512)S(1)}, f32[512]{0:T(512)}, u32[]{:S(2)}) copy-start(f32[512]{0:T(512)} %param.24) | copy-start | bytes 6148
  9.8 0.9 copy-start.6
  14.4 0.7 copy-start.7
  14.4 0.7 copy-start.8
  14.4 0.7 copy-start.9
  15.8 78.4 %reduce-scatter.3.cloned.1.call-start = ((), (), s32[]{:S(2)}) async-start(), calls=%async_computation.3 | async-start | bytes 1310720 | tf_op jit(solution)/shard_map/reduce_scatter | solution.py:162
  59.8 0.9 copy-start.2
  60.7 1.6 copy-start.3
  62.3 1.2 copy-start.4
  63.5 1.1 copy-start.5
  64.7 30.8 %copy-start.10 = (f32[2048]{0:T(1024)S(1)}, f32[2048]{0:T(1024)}, u32[]{:S(2)}) copy-start(f32[2048]{0:T(1024)} %param.27) | copy-start | bytes 24580
  64.7 31.7 %copy-start.13 = (s32[2,64,6]{1,0,2:T(2,128)S(1)}, s32[2,64,6]{1,0,2:T(2,128)}, u32[]{:S(2)}) copy-start(s32[2,64,6]{1,0,2:T(2,128)} %param.19) | copy-start | bytes 9220
  69.3 1.0 copy-start.1
  70.3 77.0 %all-gather.6.cloned.1.call-start = ((), (), s32[]{:S(2)}) async-start(), calls=%async_computation.4 | async-start | bytes 4456448 | tf_op jit(solution)/shard_map/all_gather | solution.py:166
  96.3 157.8 %reduce-scatter.5.cloned.1.call-start = ((), (), s32[]{:S(2)}) async-start(), calls=%async_computation.5 | async-start | bytes 4456448 | tf_op jit(solution)/shard_map/reduce_scatter | solution.py:186
  147.3 3.6 %copy-start.14 = (bf16[1,2048,768]{2,1,0:T(8,128)(2,1)S(1)}, bf16[1,2048,768]{2,1,0:T(8,128)(2,1)}, u32[]{:S(2)}) copy-start(bf16[1,2048,768]{2,1,0:T(8,128)(2,1)} %param.32) | copy-start | bytes 9437188
Sparse Core Ops, SparseCore 0:
  15.9 41.4 all-gather.3
  70.4 23.7 reduce-scatter.2
  96.6 50.6 all-gather.5
  183.3 70.8 reduce-scatter.4

commit v2 on v1

v2 whole, which is shorter than its diff:
```python
import math

import jax
import jax.numpy as jnp
from jax import lax
from jax.experimental import pallas as pl
from jax.experimental.pallas import tpu as pltpu
from jax.sharding import PartitionSpec as P

NOPE = 128
ROPE = 64
VDIM = 128
LATENT = 512
SEGS = 4
EPS = 1e-06
BF16 = jnp.bfloat16
F32 = jnp.float32


def rms_scale(values, gain_vec):
    values = values.astype(F32)
    return values * lax.rsqrt(jnp.mean(values * values, axis=-1, keepdims=True) + EPS) * gain_vec


def rotary_tables(positions):
    half_width = ROPE // 2
    frequency = 10000.0 ** (-jnp.arange(half_width, dtype=F32) / half_width)
    angles = positions.astype(F32)[:, None] * frequency[None, :]
    cosine = jnp.cos(angles)
    sine = jnp.sin(angles)
    return jnp.concatenate([cosine, cosine], axis=1), jnp.concatenate([-sine, sine], axis=1)


def turned(values, cosine, sine):
    half_width = values.shape[-1] // 2
    swapped = jnp.concatenate([values[:, half_width:], values[:, :half_width]], axis=1)
    return values * cosine + swapped * sine


def silu_mul(gate, up):
    return gate / (1.0 + jnp.exp(-gate)) * up


def layer_kernel(
    normed_ref, own_lat_ref, cos_ref, sin_ref, low_ref, high_ref, input_ref, gain_ref, combine_ref,
    wq_hbm, wkv_hbm, wo_hbm, sg_hbm, su_hbm, sd_hbm, eg_hbm, eu_hbm, ed_hbm,
    out_ref,
    wq, wkv, wo, sg, su, sd, eg, eu, ed,
    keys, att, rows, act, shared_act, partial, core_in, y_out, y_in, ring_out, ring_in, own_sum, residual,
    w_sem, lat_s, lat_r, latc_s, latc_r, zf_s, zf_r, yf_s, yf_r, cf_s, cf_r,
    rc_s, rc_r, ry_s, ry_r, rz_s, rz_r,
):
    n_tok = lax.axis_size("tok")
    n_mdl = lax.axis_size("mdl")
    n_y = n_mdl // 2
    section = lax.axis_index("section")
    t = lax.axis_index("tok")
    m = lax.axis_index("mdl")
    y, c = m // 2, m % 2
    tok_dev, width = normed_ref.shape
    row_dev = tok_dev // n_mdl
    half = tok_dev // 2
    back = keys.shape[0] // tok_dev - 1
    heads = wo.shape[0] // VDIM
    experts = n_tok * n_mdl
    mesh_id = pl.DeviceIdType.MESH
    sibling = (section, t, y * 2 + 1 - c)

    def tok_peer(step):
        return (section, lax.rem(t + step + n_tok, n_tok), m)

    def rank_y(step):
        return lax.rem(y + step + n_y, n_y) * 2 + c

    def y_peer(step):
        return (section, t, rank_y(step))

    def at_rank(rank):
        return pl.ds(pl.multiple_of(rank * row_dev, row_dev), row_dev)

    def remote(source, target, send_sem, recv_sem, device):
        return pltpu.make_async_remote_copy(
            src_ref=source, dst_ref=target, send_sem=send_sem, recv_sem=recv_sem,
            device_id=device, device_id_type=mesh_id,
        )

    loads = [
        pltpu.make_async_copy(src, dst, w_sem.at[i])
        for i, (src, dst) in enumerate(
            [(wq_hbm, wq), (wkv_hbm, wkv), (wo_hbm, wo), (sg_hbm, sg), (su_hbm, su), (sd_hbm, sd),
             (eg_hbm.at[0], eg), (eu_hbm.at[0], eu), (ed_hbm.at[0], ed)]
        )
    ]
    for load in loads:
        load.start()

    barrier = pltpu.get_barrier_semaphore()
    for step in range(1, back + 1):
        pl.semaphore_signal(barrier, inc=1, device_id=tok_peer(-step), device_id_type=mesh_id)
    pl.semaphore_signal(barrier, inc=1, device_id=sibling, device_id_type=mesh_id)
    for step in range(1, n_y):
        pl.semaphore_signal(barrier, inc=1, device_id=y_peer(-step), device_id_type=mesh_id)
    pl.semaphore_wait(barrier, back + n_y)

    def key_rows(step, core):
        return keys.at[pl.ds(pl.multiple_of(step * tok_dev + core * half, half), half)]

    def lat_copy(step):
        return remote(own_lat_ref, key_rows(step, c), lat_s.at[step], lat_r.at[step], tok_peer(step))

    def lat_core_copy(step):
        source = own_lat_ref if step == 0 else key_rows(step, c)
        return remote(source, key_rows(step, c), latc_s.at[step], latc_r.at[step], sibling)

    for step in range(back, 0, -1):
        lat_copy(step).start()
    lat_core_copy(0).start()
    keys[pl.ds(pl.multiple_of(c * half, half), half), :] = own_lat_ref[...]
    loads[0].wait()
    queries = jnp.dot(normed_ref[...], wq[...], preferred_element_type=F32)
    for step in range(1, back + 1):
        lat_copy(step).wait_recv()
        lat_core_copy(step).start()
    for step in range(back + 1):
        lat_core_copy(step).wait_recv()
    loads[1].wait()

    qk = NOPE + ROPE
    span = keys.shape[0]
    column = lax.broadcasted_iota(jnp.int32, (tok_dev, span), 1)
    key_index = t * tok_dev + column
    for step in range(1, back + 1):
        key_index = key_index - jnp.where(column >= step * tok_dev, 2 * tok_dev, 0)
    allowed = (key_index >= low_ref[...]) & (key_index <= high_ref[...])
    contract = (((1,), (1,)), ((), ()))
    cosine, sine = cos_ref[...], sin_ref[...]
    scale = 1.0 / math.sqrt(qk)
    for h in range(heads):
        kv = jnp.dot(
            keys[:, :LATENT], wkv[:, h * (NOPE + VDIM) : (h + 1) * (NOPE + VDIM)],
            preferred_element_type=F32,
        ).astype(BF16)
        q_nope = queries[:, h * qk : h * qk + NOPE].astype(BF16)
        q_rope = turned(queries[:, h * qk + NOPE : (h + 1) * qk], cosine, sine).astype(BF16)
        scores = lax.dot_general(q_nope, kv[:, :NOPE], contract, preferred_element_type=F32)
        scores += lax.dot_general(q_rope, keys[:, LATENT:], contract, preferred_element_type=F32)
        scores = jnp.where(allowed, scores * scale, -1e30)
        top = jnp.max(scores, axis=1, keepdims=True)
        weights = jnp.where(allowed, jnp.exp(scores - top), 0.0)
        total = jnp.sum(weights, axis=1, keepdims=True)
        summed = jnp.dot(weights.astype(BF16), kv[:, NOPE:], preferred_element_type=F32)
        att[:, h * VDIM : (h + 1) * VDIM] = (summed / total).astype(BF16)
    loads[2].wait()

    chunk = 512

    def chunk_of(i, size):
        return pl.ds(pl.multiple_of(i * size, size), size)

    @pl.loop(0, width // chunk)
    def _(i):
        partial[n_tok, :, chunk_of(i, chunk)] = jnp.dot(
            att[...], wo[:, chunk_of(i, chunk)], preferred_element_type=F32
        ).astype(BF16)

    def core_copy(k, j):
        other = lax.rem(y + j, n_y) * 2 + 1 - c
        return remote(
            partial.at[k, at_rank(other)], core_in.at[k, j], rc_s.at[k, j], rc_r.at[k, j], sibling
        )

    def y_copy(k, j):
        return remote(
            y_out.at[k, j - 1], y_in.at[k, j - 1], ry_s.at[k, j], ry_r.at[k, j], y_peer(j)
        )

    def start_core(k):
        for j in range(n_y):
            core_copy(k, j).start()

    def core_to_y(k):
        for j in range(n_y):
            core_copy(k, j).wait_recv()
        for j in range(1, n_y):
            y_out[k, j - 1] = (
                partial[k, at_rank(rank_y(j)), :].astype(F32) + core_in[k, j].astype(F32)
            ).astype(BF16)
            y_copy(k, j).start()

    def y_total(k):
        for j in range(1, n_y):
            y_copy(k, j).wait_recv()
        total = partial[k, at_rank(m), :].astype(F32) + core_in[k, 0].astype(F32)
        for j in range(1, n_y):
            total += y_in[k, j - 1].astype(F32)
        return total

    start_core(n_tok)
    core_to_y(n_tok)
    res = (input_ref[...].astype(F32) + y_total(n_tok)).astype(BF16)
    residual[...] = res
    rows[0, at_rank(m), :width] = rms_scale(res, gain_ref[...]).astype(BF16)
    combine = combine_ref[...]
    high_part = combine.astype(BF16)
    extra = combine.shape[1]
    rows[0, at_rank(m), width : width + extra] = high_part
    rows[0, at_rank(m), width + extra :] = (combine - high_part.astype(F32)).astype(BF16)

    def z_row_copy(k):
        return remote(
            rows.at[k, at_rank(m)], rows.at[k + 1, at_rank(m)], zf_s.at[k], zf_r.at[k], tok_peer(1)
        )

    def y_row_copy(k, j):
        place = rows.at[k, at_rank(m)]
        return remote(place, place, yf_s.at[k, j], yf_r.at[k, j], y_peer(j))

    def core_row_copy(k, j):
        place = rows.at[k, at_rank(rank_y(-j))]
        return remote(place, place, cf_s.at[k, j], cf_r.at[k, j], sibling)

    def forward(k):
        for j in range(1, n_y):
            y_row_copy(k, j).start()
        core_row_copy(k, 0).start()

    def forward_core(k):
        for j in range(1, n_y):
            y_row_copy(k, j).wait_recv()
            core_row_copy(k, j).start()

    def ring_copy(k):
        return remote(ring_out.at[k], ring_in.at[k], rz_s.at[k], rz_r.at[k], tok_peer(1))

    def to_ring(k):
        total = y_total(k)

        @pl.when(k == 0)
        def _():
            own_sum[...] = total

        @pl.when(k == 1)
        def _():
            ring_out[k] = total.astype(BF16)
            ring_copy(k).start()

        @pl.when(k >= 2)
        def _():
            ring_copy(k - 1).wait_recv()
            ring_out[k] = (total + ring_in[k - 1].astype(F32)).astype(BF16)
            ring_copy(k).start()

    z_row_copy(0).start()
    forward(0)
    forward_core(0)
    for load in loads[3:]:
        load.wait()

    block = 256
    expert = t * n_mdl + m
    lane = lax.broadcasted_iota(jnp.int32, (tok_dev, 2 * extra), 1)
    mine = (lane == expert) | (lane == expert + extra)

    @pl.loop(0, n_tok)
    def _(k):
        for j in range(n_y):
            core_row_copy(k, j).wait_recv()

        @pl.when(k + 1 < n_tok)
        def _():
            z_row_copy(k).wait_recv()

            @pl.when(k + 2 < n_tok)
            def _():
                z_row_copy(k + 1).start()

            forward(k + 1)

        row_weight = jnp.sum(
            jnp.where(mine, rows[k, :, width:].astype(F32), 0.0), axis=1, keepdims=True
        )

        @pl.loop(0, eg.shape[1] // block)
        def _(i):
            group = rows[k, :, :width]
            gate = jnp.dot(group, eg[:, chunk_of(i, block)], preferred_element_type=F32)
            up = jnp.dot(group, eu[:, chunk_of(i, block)], preferred_element_type=F32)
            act[:, chunk_of(i, block)] = (silu_mul(gate, up) * row_weight).astype(BF16)

        @pl.when(k == 0)
        def _():
            @pl.loop(0, sg.shape[1] // block)
            def _(i):
                group = rows[0, :, :width]
                gate = jnp.dot(group, sg[:, chunk_of(i, block)], preferred_element_type=F32)
                up = jnp.dot(group, su[:, chunk_of(i, block)], preferred_element_type=F32)
                shared_act[:, chunk_of(i, block)] = silu_mul(gate, up).astype(BF16)

            @pl.loop(0, width // chunk)
            def _(i):
                partial[k, :, chunk_of(i, chunk)] = (
                    jnp.dot(act[...], ed[:, chunk_of(i, chunk)], preferred_element_type=F32)
                    + jnp.dot(shared_act[...], sd[:, chunk_of(i, chunk)], preferred_element_type=F32)
                ).astype(BF16)

        @pl.when(k > 0)
        def _():
            @pl.loop(0, width // chunk)
            def _(i):
                partial[k, :, chunk_of(i, chunk)] = jnp.dot(
                    act[...], ed[:, chunk_of(i, chunk)], preferred_element_type=F32
                ).astype(BF16)

        start_core(k)

        @pl.when(k >= 1)
        def _():
            to_ring(k - 1)

        @pl.when(k + 1 < n_tok)
        def _():
            forward_core(k + 1)

        core_to_y(k)

    to_ring(jnp.int32(n_tok - 1))
    ring_copy(n_tok - 1).wait_recv()
    out_ref[...] = (
        residual[...].astype(F32) + own_sum[...] + ring_in[n_tok - 1].astype(F32)
    ).astype(BF16)

    for step in range(1, back + 1):
        lat_copy(step).wait_send()
    for step in range(back + 1):
        lat_core_copy(step).wait_send()

    @pl.loop(0, n_tok + 1)
    def _(k):
        for j in range(n_y):
            core_copy(k, j).wait_send()
        for j in range(1, n_y):
            y_copy(k, j).wait_send()

    @pl.loop(0, n_tok)
    def _(k):
        for j in range(n_y):
            core_row_copy(k, j).wait_send()
        for j in range(1, n_y):
            y_row_copy(k, j).wait_send()

    @pl.loop(0, n_tok - 1)
    def _(k):
        z_row_copy(k).wait_send()
        ring_copy(k + 1).wait_send()


def shards(
    layer_input, segment_ids, route_ids, route_weights, attn_gain, w_query, w_kv_down, latent_gain,
    w_kv_up, w_out, ffn_gain, w_shared_gate, w_shared_up, w_shared_down, w_expert_gate, w_expert_up,
    w_expert_down,
):
    n_tok = lax.axis_size("tok")
    n_mdl = lax.axis_size("mdl")
    n_y = n_mdl // 2
    batch = lax.axis_index("section")
    tok_rank = lax.axis_index("tok")
    mdl_rank = lax.axis_index("mdl")
    micro_count, tok_dev, width = layer_input.shape
    assert micro_count == lax.axis_size("section") and w_expert_gate.shape[0] == 1
    row_dev = tok_dev // n_mdl
    half = tok_dev // 2
    pack = segment_ids.shape[1]
    expert_total = n_tok * n_mdl
    back = min(n_tok - 1, -(-(pack // 2) // tok_dev))
    rows_in = lax.dynamic_index_in_dim(layer_input, batch, 0, keepdims=False)
    segment_row = lax.dynamic_index_in_dim(segment_ids, batch, 0, keepdims=False)
    chosen = lax.dynamic_index_in_dim(route_ids, batch, 0, keepdims=False)
    chosen_weights = lax.dynamic_index_in_dim(route_weights, batch, 0, keepdims=False)
    extra = -(-expert_total // 128) * 128
    labels = jnp.arange(extra, dtype=jnp.int32)
    combining = jnp.sum(
        jnp.where(chosen[:, :, None] == labels, chosen_weights[:, :, None], 0.0), axis=1
    )
    query_start = tok_rank * tok_dev
    query_seg = lax.dynamic_slice_in_dim(segment_row, query_start, tok_dev)
    firsts = jnp.sum((segment_row[None, :] < query_seg[:, None]).astype(jnp.int32), axis=1)
    query_index = query_start + jnp.arange(tok_dev, dtype=jnp.int32)
    cosine, sine = rotary_tables(query_index - firsts)
    own = mdl_rank * row_dev
    lead = (mdl_rank % 2) * half
    normed = rms_scale(rows_in, attn_gain).astype(BF16)
    half_normed = lax.dynamic_slice_in_dim(normed, lead, half)
    compressed = jnp.dot(half_normed, w_kv_down, preferred_element_type=F32)
    latent = rms_scale(compressed[:, :LATENT], latent_gain).astype(BF16)
    key_rope = turned(
        compressed[:, LATENT:],
        lax.dynamic_slice_in_dim(cosine, lead, half),
        lax.dynamic_slice_in_dim(sine, lead, half),
    ).astype(BF16)
    own_lat = jnp.concatenate([latent, key_rope], axis=1)
    own_input = lax.dynamic_slice_in_dim(rows_in, own, row_dev)
    inputs = [
        normed, own_lat, cosine, sine, firsts[:, None], query_index[:, None], own_input,
        ffn_gain[None, :], combining,
    ]
    weights = [
        w_query, w_kv_up, w_out, w_shared_gate, w_shared_up, w_shared_down, w_expert_gate,
        w_expert_up, w_expert_down,
    ]
    held = [pltpu.VMEM(w.shape[-2:], BF16) for w in weights]
    dma = pltpu.SemaphoreType.DMA
    result = pl.pallas_call(
        layer_kernel,
        out_shape=jax.ShapeDtypeStruct((row_dev, width), BF16),
        in_specs=[pl.BlockSpec(memory_space=pltpu.VMEM)] * len(inputs)
        + [pl.BlockSpec(memory_space=pl.ANY)] * len(weights),
        out_specs=pl.BlockSpec(memory_space=pltpu.VMEM),
        scratch_shapes=held
        + [
            pltpu.VMEM(((back + 1) * tok_dev, LATENT + ROPE), BF16),
            pltpu.VMEM((tok_dev, w_out.shape[0]), BF16),
            pltpu.VMEM((n_tok, tok_dev, width + 2 * extra), BF16),
            pltpu.VMEM((tok_dev, w_expert_gate.shape[2]), BF16),
            pltpu.VMEM((tok_dev, w_shared_gate.shape[1]), BF16),
            pltpu.VMEM((n_tok + 1, tok_dev, width), BF16),
            pltpu.VMEM((n_tok + 1, n_y, row_dev, width), BF16),
            pltpu.VMEM((n_tok + 1, n_y - 1, row_dev, width), BF16),
            pltpu.VMEM((n_tok + 1, n_y - 1, row_dev, width), BF16),
            pltpu.VMEM((n_tok, row_dev, width), BF16),
            pltpu.VMEM((n_tok, row_dev, width), BF16),
            pltpu.VMEM((row_dev, width), F32),
            pltpu.VMEM((row_dev, width), BF16),
            dma((len(weights),)),
        ]
        + [dma((back + 1,))] * 4
        + [dma((n_tok,))] * 2
        + [dma((n_tok, n_y))] * 4
        + [dma((n_tok + 1, n_y))] * 4
        + [dma((n_tok,))] * 2,
        compiler_params=pltpu.CompilerParams(
            collective_id=0, has_side_effects=True, vmem_limit_bytes=60 * 2**20
        ),
        cost_estimate=pl.CostEstimate(
            flops=14 * 10**9, bytes_accessed=25 * 10**6, transcendentals=2 * 10**6
        ),
    )(*inputs, *weights)
    return result[None]


def solution(mesh):
    in_specs = (
        P(None, "tok", None),
        P(),
        P(None, ("tok", "mdl"), None),
        P(None, ("tok", "mdl"), None),
        P(),
        P(None, "mdl"),
        P(),
        P(),
        P(None, "mdl"),
        P("mdl", None),
        P(),
        P(None, "mdl"),
        P(None, "mdl"),
        P("mdl", None),
        P(("tok", "mdl"), None, None),
        P(("tok", "mdl"), None, None),
        P(("tok", "mdl"), None, None),
    )
    out_specs = P("section", ("tok", "mdl"), None)
    return jax.shard_map(shards, mesh=mesh, in_specs=in_specs, out_specs=out_specs, check_vma=False)
```

time: 263 us -> 117 us (0.44)
  waiting for transfers between devices: 158 us -> 0 us
  Pallas kernels: 4.63 us -> 103 us
  matrix products: 36.4 us -> 0.93 us
  blocking collectives: 21.2 us -> 0 us
  between operations: 13.4 us -> 0.15 us
  other arithmetic: 16.7 us -> 7.29 us
  local copies, waits for them, and re-layouts: 12.2 us -> 5.4 us
    pallas_call x1, Pallas kernels: 4.63 us -> 103 us  [shards(): pl.pallas_call(layer_kernel, out_shape=jax.ShapeDtypeStruct((row_dev, wid...]
    reduce_scatter x2 -> x0, waiting for transfers between devices: 94.8 us -> none  [the longest x1 71 us: shards(): lax.psum_scatter(outgoing.astype(BF16), ('tok', 'mdl'), scatter_dimension...]
    all_gather x2 -> x0, waiting for transfers between devices: 62.9 us -> none  [the longest x1 35.5 us: shards(): lax.all_gather(jnp.concatenate([latent, key_rope], axis=1), ('tok', 'mdl'...]
    dot_general x6 -> x1, matrix products: 36.4 us -> 0.93 us  [shards(): compressed = jnp.dot(half_normed, w_kv_down, preferred_element_type=F32)]
    all_gather x1 -> x0, blocking collectives: 21.2 us -> none  [shards(): lax.all_gather(combining, ('tok', 'mdl'), axis=0, tiled=True)]
    convert_element_type x2 -> x1, other arithmetic: 6.83 us -> 0.01 us  [rotary_tables(): angles = positions.astype(F32)[:, None] * frequency[None, :]]
    unnamed x33 -> x15, local copies, waits for them, and re-layouts: 8 us -> 2.68 us
  transfers between devices with their start and end apart: 4 -> 0, of which waited for: 4 -> 0; matrix products, arithmetic and copies ran while one was open for 3% -> 0% of each run, Pallas kernels for 0% -> 0%
where the time goes in v2:
time: 117 us
  Pallas kernels  103 us (88%)
  other arithmetic  7.29 us (6%)
  local copies, waits for them, and re-layouts  5.4 us (5%)
    pallas_call x1, Pallas kernels, shards(): pl.pallas_call(layer_kernel, out_shape=jax.ShapeDtypeStruct((row_dev, wid...  103 us
    unnamed x15, local copies, waits for them, and re-layouts  2.68 us

profile of v2, /device:TPU:0, one launch (start us, length us, event | category | flops | bytes accessed | tf_op | source)
XLA Modules:
  0.0 116.7 jit_solution(17516301646176413116)
XLA Ops:
  0.0 0.0 copy-start
  0.0 1.7 %fusion = f32[256]{0:T(256)S(1)} fusion(bf16[2,256,2048]{2,1,0:T(8,128)(2,1)} %param.17, s32[]{:T(128)S(6)} %select_n.38), kind=kLoop, calls=%fused_computation.2 | loop fusion | flops 1572608 | bytes 1049604 | tf_op jit(solution)/shard_map/reduce_sum | solution.py:22
  1.7 1.6 %fusion.2.normed_ref = bf16[256,2048]{1,0:T(8,128)(2,1)S(1)} fusion(f32[2048]{0:T(1024)} %param.21, f32[256]{0:T(256)S(1)} %add_rsqrt_fusion, bf16[2,256,2048]{2,1,0:T(8,128)(2,1)} %param.17, s32[]{:T(128)S(6)} %select_n.38), kind=kLoop, calls=%fused_computation.4 | loop fusion | flops 2097152 | bytes 2106372 | tf_op jit(solution)/shard_map/convert_element_type | solution.py:391
  3.2 0.0 copy-start.1
  3.2 1.0 copy-done.1
  4.2 0.0 copy-done
  4.2 0.0 copy-start.3
  4.2 0.0 copy-start.2
  4.2 0.9 fusion.3
  5.2 0.0 copy-start.4
  5.2 0.0 copy-start.5
  5.2 0.1 multiply_reduce_fusion
  5.3 0.0 copy-done.3
  5.3 0.1 multiply_convert_fusion
  5.4 0.1 fusion.13
  5.5 0.0 copy-done.2
  5.5 0.1 dynamic_slice.36
  5.6 0.2 convert_reduce_fusion
  5.9 0.5 multiply_cosine_fusion
  6.4 0.1 fusion.8
  6.5 0.7 pad_maximum_fusion.own_lat_ref
  7.2 0.8 pad_maximum_fusion.1
  8.1 0.8 copy.45.low_ref
  8.9 1.7 %dynamic-slice_bitcast_fusion.input_ref = bf16[64,2048]{1,0:T(8,128)(2,1)} fusion(bf16[2,256,2048]{2,1,0:T(8,128)(2,1)} %param.17, s32[]{:T(128)S(6)} %select_n.41, s32[]{:T(128)S(6)} %select_n.45), kind=kLoop, calls=%fused_computation.8 | loop fusion | bytes 524296 | tf_op jit(solution)/shard_map/dynamic_slice | solution.py:401
  10.6 0.0 copy-done.4
  10.6 0.0 copy-done.5
  10.7 0.8 select_reduce_fusion.combine_ref
  11.4 0.7 iota_add_fusion.high_ref
  12.1 103.0 %shard_map.163 = bf16[64,2048]{1,0:T(8,128)(2,1)} custom-call(bf16[256,2048]{1,0:T(8,128)(2,1)} %copy-done.1, bf16[128,576]{1,0:T(8,128)(2,1)} %pad_maximum_fusion.own_lat_ref, f32[256,64]{1,0:T(8,128)} %get-tuple-element.10.cos_ref, f32[256,64]{1,0:T(8,128)} %get-tuple-element.11.sin_ref, s32[256,1]{1,0:T(8,128)} %copy.45.low_ref, ...), custom_call_target="tpu_custom_call" | custom-call | flops 14000000000 | bytes 25000000 | tf_op jit(solution)/shard_map/pallas_call | solution.py:412
  115.1 1.7 %copy.54 = bf16[1,64,2048]{2,1,0:T(8,128)(2,1)} copy(bf16[1,64,2048]{2,1,0:T(8,128)(2,1)} %bitcast.18) | data formatting | bytes 524288
  (9 shorter events, 0.1 us)
Async XLA Ops:
  0.0 4.2 %copy-start = (bf16[2048,576]{0,1:T(8,128)(2,1)S(1)}, bf16[2048,576]{0,1:T(8,128)(2,1)}, u32[]{:S(2)}) copy-start(bf16[2048,576]{0,1:T(8,128)(2,1)} %param.23) | copy-start | bytes 7077892
  3.2 1.0 copy-start.1
  4.2 1.1 copy-start.3
  4.2 1.3 %copy-start.2 = (s32[2,1024]{1,0:T(2,128)S(1)}, s32[2,1024]{1,0:T(2,128)}, u32[]{:S(2)}) copy-start(s32[2,1024]{1,0:T(2,128)} %param.18) | copy-start | bytes 24580
  5.2 5.4 %copy-start.4 = (f32[2,64,6]{1,0,2:T(2,128)S(1)}, f32[2,64,6]{1,0,2:T(2,128)}, u32[]{:S(2)}) copy-start(f32[2,64,6]{1,0,2:T(2,128)} %param.20) | copy-start | bytes 9220
  5.2 5.4 %copy-start.5 = (s32[2,64,6]{1,0,2:T(2,128)S(1)}, s32[2,64,6]{1,0,2:T(2,128)}, u32[]{:S(2)}) copy-start(s32[2,64,6]{1,0,2:T(2,128)} %param.19) | copy-start | bytes 9220

commit v3 on v2

--- a/solution.py
+++ b/solution.py
@@ -24,11 +24,10 @@
 
 def rotary_tables(positions):
     half_width = ROPE // 2
-    frequency = 10000.0 ** (-jnp.arange(half_width, dtype=F32) / half_width)
+    lane = jnp.arange(ROPE, dtype=jnp.int32)
+    frequency = 10000.0 ** (-(lane % half_width).astype(F32) / half_width)
     angles = positions.astype(F32)[:, None] * frequency[None, :]
-    cosine = jnp.cos(angles)
-    sine = jnp.sin(angles)
-    return jnp.concatenate([cosine, cosine], axis=1), jnp.concatenate([-sine, sine], axis=1)
+    return jnp.cos(angles), jnp.where(lane < half_width, -1.0, 1.0) * jnp.sin(angles)
 
 
 def turned(values, cosine, sine):
@@ -42,11 +41,11 @@
 
 
 def layer_kernel(
-    normed_ref, own_lat_ref, cos_ref, sin_ref, low_ref, high_ref, input_ref, gain_ref, combine_ref,
-    wq_hbm, wkv_hbm, wo_hbm, sg_hbm, su_hbm, sd_hbm, eg_hbm, eu_hbm, ed_hbm,
+    cos_ref, sin_ref, low_ref, attn_gain_ref, lat_gain_ref, gain_ref, combine_ref,
+    x_hbm, wd_hbm, wq_hbm, wkv_hbm, wo_hbm, sg_hbm, su_hbm, sd_hbm, eg_hbm, eu_hbm, ed_hbm,
     out_ref,
-    wq, wkv, wo, sg, su, sd, eg, eu, ed,
-    keys, att, rows, act, shared_act, partial, core_in, y_out, y_in, ring_out, ring_in, own_sum, residual,
+    x_in, normed, wd, wq, wkv, wo, sg, su, sd, eg, eu, ed,
+    keys, att, rows, act, shared_act, partial, core_in, y_out, y_in, ring_out, ring_in, residual,
     w_sem, lat_s, lat_r, latc_s, latc_r, zf_s, zf_r, yf_s, yf_r, cf_s, cf_r,
     rc_s, rc_r, ry_s, ry_r, rz_s, rz_r,
 ):
@@ -57,7 +56,7 @@
     t = lax.axis_index("tok")
     m = lax.axis_index("mdl")
     y, c = m // 2, m % 2
-    tok_dev, width = normed_ref.shape
+    tok_dev, width = x_in.shape
     row_dev = tok_dev // n_mdl
     half = tok_dev // 2
     back = keys.shape[0] // tok_dev - 1
@@ -87,7 +86,7 @@
     loads = [
         pltpu.make_async_copy(src, dst, w_sem.at[i])
         for i, (src, dst) in enumerate(
-            [(wq_hbm, wq), (wkv_hbm, wkv), (wo_hbm, wo), (sg_hbm, sg), (su_hbm, su), (sd_hbm, sd),
+            [(x_hbm.at[section], x_in), (wd_hbm, wd), (wq_hbm, wq), (wkv_hbm, wkv), (wo_hbm, wo), (sg_hbm, sg), (su_hbm, su), (sd_hbm, sd),
              (eg_hbm.at[0], eg), (eu_hbm.at[0], eu), (ed_hbm.at[0], ed)]
         )
     ]
@@ -95,43 +94,54 @@
         load.start()
 
     barrier = pltpu.get_barrier_semaphore()
-    for step in range(1, back + 1):
-        pl.semaphore_signal(barrier, inc=1, device_id=tok_peer(-step), device_id_type=mesh_id)
+    pl.semaphore_signal(barrier, inc=1, device_id=tok_peer(-1), device_id_type=mesh_id)
     pl.semaphore_signal(barrier, inc=1, device_id=sibling, device_id_type=mesh_id)
     for step in range(1, n_y):
         pl.semaphore_signal(barrier, inc=1, device_id=y_peer(-step), device_id_type=mesh_id)
-    pl.semaphore_wait(barrier, back + n_y)
+    loads[0].wait()
+    normed[...] = rms_scale(x_in[...], attn_gain_ref[...]).astype(BF16)
+    lead = pl.ds(pl.multiple_of(c * half, half), half)
+    loads[1].wait()
+    compressed = jnp.dot(normed[lead, :], wd[...], preferred_element_type=F32)
+    keys[lead, :LATENT] = rms_scale(compressed[:, :LATENT], lat_gain_ref[...]).astype(BF16)
+    keys[lead, LATENT:] = turned(
+        compressed[:, LATENT:], cos_ref[lead, :], sin_ref[lead, :]
+    ).astype(BF16)
+    pl.semaphore_wait(barrier, 1 + n_y)
 
     def key_rows(step, core):
         return keys.at[pl.ds(pl.multiple_of(step * tok_dev + core * half, half), half)]
 
     def lat_copy(step):
-        return remote(own_lat_ref, key_rows(step, c), lat_s.at[step], lat_r.at[step], tok_peer(step))
+        return remote(
+            key_rows(step - 1, c), key_rows(step, c), lat_s.at[step], lat_r.at[step], tok_peer(1)
+        )
 
     def lat_core_copy(step):
-        source = own_lat_ref if step == 0 else key_rows(step, c)
-        return remote(source, key_rows(step, c), latc_s.at[step], latc_r.at[step], sibling)
-
-    for step in range(back, 0, -1):
-        lat_copy(step).start()
+        place = key_rows(step, c)
+        return remote(place, place, latc_s.at[step], latc_r.at[step], sibling)
+
+    lat_copy(1).start()
     lat_core_copy(0).start()
-    keys[pl.ds(pl.multiple_of(c * half, half), half), :] = own_lat_ref[...]
-    loads[0].wait()
-    queries = jnp.dot(normed_ref[...], wq[...], preferred_element_type=F32)
+    loads[2].wait()
+    queries = jnp.dot(normed[...], wq[...], preferred_element_type=F32)
     for step in range(1, back + 1):
         lat_copy(step).wait_recv()
+        if step < back:
+            lat_copy(step + 1).start()
         lat_core_copy(step).start()
     for step in range(back + 1):
         lat_core_copy(step).wait_recv()
-    loads[1].wait()
+    loads[3].wait()
 
     qk = NOPE + ROPE
     span = keys.shape[0]
     column = lax.broadcasted_iota(jnp.int32, (tok_dev, span), 1)
     key_index = t * tok_dev + column
+    query_index = t * tok_dev + lax.broadcasted_iota(jnp.int32, (tok_dev, span), 0)
     for step in range(1, back + 1):
         key_index = key_index - jnp.where(column >= step * tok_dev, 2 * tok_dev, 0)
-    allowed = (key_index >= low_ref[...]) & (key_index <= high_ref[...])
+    allowed = (key_index >= low_ref[...]) & (key_index <= query_index)
     contract = (((1,), (1,)), ((), ()))
     cosine, sine = cos_ref[...], sin_ref[...]
     scale = 1.0 / math.sqrt(qk)
@@ -150,7 +160,7 @@
         total = jnp.sum(weights, axis=1, keepdims=True)
         summed = jnp.dot(weights.astype(BF16), kv[:, NOPE:], preferred_element_type=F32)
         att[:, h * VDIM : (h + 1) * VDIM] = (summed / total).astype(BF16)
-    loads[2].wait()
+    loads[4].wait()
 
     chunk = 512
 
@@ -197,7 +207,7 @@
 
     start_core(n_tok)
     core_to_y(n_tok)
-    res = (input_ref[...].astype(F32) + y_total(n_tok)).astype(BF16)
+    res = (x_in[at_rank(m), :].astype(F32) + y_total(n_tok)).astype(BF16)
     residual[...] = res
     rows[0, at_rank(m), :width] = rms_scale(res, gain_ref[...]).astype(BF16)
     combine = combine_ref[...]
@@ -235,10 +245,6 @@
     def to_ring(k):
         total = y_total(k)
 
-        @pl.when(k == 0)
-        def _():
-            own_sum[...] = total
-
         @pl.when(k == 1)
         def _():
             ring_out[k] = total.astype(BF16)
@@ -253,7 +259,7 @@
     z_row_copy(0).start()
     forward(0)
     forward_core(0)
-    for load in loads[3:]:
+    for load in loads[5:]:
         load.wait()
 
     block = 256
@@ -313,20 +319,24 @@
 
         start_core(k)
 
+        @pl.when(k >= 2)
+        def _():
+            to_ring(k - 1)
+
+        @pl.when(k + 1 < n_tok)
+        def _():
+            forward_core(k + 1)
+
         @pl.when(k >= 1)
         def _():
-            to_ring(k - 1)
-
-        @pl.when(k + 1 < n_tok)
-        def _():
-            forward_core(k + 1)
-
-        core_to_y(k)
-
+            core_to_y(k)
+
+    core_to_y(0)
     to_ring(jnp.int32(n_tok - 1))
+    own_sum = y_total(0)
     ring_copy(n_tok - 1).wait_recv()
     out_ref[...] = (
-        residual[...].astype(F32) + own_sum[...] + ring_in[n_tok - 1].astype(F32)
+        residual[...].astype(F32) + own_sum + ring_in[n_tok - 1].astype(F32)
     ).astype(BF16)
 
     for step in range(1, back + 1):
@@ -364,15 +374,12 @@
     n_y = n_mdl // 2
     batch = lax.axis_index("section")
     tok_rank = lax.axis_index("tok")
-    mdl_rank = lax.axis_index("mdl")
     micro_count, tok_dev, width = layer_input.shape
     assert micro_count == lax.axis_size("section") and w_expert_gate.shape[0] == 1
     row_dev = tok_dev // n_mdl
-    half = tok_dev // 2
     pack = segment_ids.shape[1]
     expert_total = n_tok * n_mdl
     back = min(n_tok - 1, -(-(pack // 2) // tok_dev))
-    rows_in = lax.dynamic_index_in_dim(layer_input, batch, 0, keepdims=False)
     segment_row = lax.dynamic_index_in_dim(segment_ids, batch, 0, keepdims=False)
     chosen = lax.dynamic_index_in_dim(route_ids, batch, 0, keepdims=False)
     chosen_weights = lax.dynamic_index_in_dim(route_weights, batch, 0, keepdims=False)
@@ -386,28 +393,16 @@
     firsts = jnp.sum((segment_row[None, :] < query_seg[:, None]).astype(jnp.int32), axis=1)
     query_index = query_start + jnp.arange(tok_dev, dtype=jnp.int32)
     cosine, sine = rotary_tables(query_index - firsts)
-    own = mdl_rank * row_dev
-    lead = (mdl_rank % 2) * half
-    normed = rms_scale(rows_in, attn_gain).astype(BF16)
-    half_normed = lax.dynamic_slice_in_dim(normed, lead, half)
-    compressed = jnp.dot(half_normed, w_kv_down, preferred_element_type=F32)
-    latent = rms_scale(compressed[:, :LATENT], latent_gain).astype(BF16)
-    key_rope = turned(
-        compressed[:, LATENT:],
-        lax.dynamic_slice_in_dim(cosine, lead, half),
-        lax.dynamic_slice_in_dim(sine, lead, half),
-    ).astype(BF16)
-    own_lat = jnp.concatenate([latent, key_rope], axis=1)
-    own_input = lax.dynamic_slice_in_dim(rows_in, own, row_dev)
     inputs = [
-        normed, own_lat, cosine, sine, firsts[:, None], query_index[:, None], own_input,
-        ffn_gain[None, :], combining,
+        cosine, sine, firsts[:, None], attn_gain[None, :], latent_gain[None, :], ffn_gain[None, :],
+        combining,
     ]
     weights = [
-        w_query, w_kv_up, w_out, w_shared_gate, w_shared_up, w_shared_down, w_expert_gate,
+        layer_input, w_kv_down, w_query, w_kv_up, w_out, w_shared_gate, w_shared_up, w_shared_down, w_expert_gate,
         w_expert_up, w_expert_down,
     ]
-    held = [pltpu.VMEM(w.shape[-2:], BF16) for w in weights]
+    held = [pltpu.VMEM((tok_dev, width), BF16)] * 2
+    held += [pltpu.VMEM(w.shape[-2:], BF16) for w in weights[1:]]
     dma = pltpu.SemaphoreType.DMA
     result = pl.pallas_call(
         layer_kernel,
@@ -428,7 +423,6 @@
             pltpu.VMEM((n_tok + 1, n_y - 1, row_dev, width), BF16),
             pltpu.VMEM((n_tok, row_dev, width), BF16),
             pltpu.VMEM((n_tok, row_dev, width), BF16),
-            pltpu.VMEM((row_dev, width), F32),
             pltpu.VMEM((row_dev, width), BF16),
             dma((len(weights),)),
         ]

time: 117 us -> 105 us (0.90)
  Pallas kernels: 103 us -> 93.2 us
  other arithmetic: 7.29 us -> 2.27 us
  local copies, waits for them, and re-layouts: 5.4 us -> 9 us
    pallas_call x1, Pallas kernels: 103 us -> 93.2 us  [shards(): pl.pallas_call(layer_kernel, out_shape=jax.ShapeDtypeStruct((row_dev, wid...]
    unnamed x15 -> x6, local copies, waits for them, and re-layouts: 2.68 us -> 6.01 us
    convert_element_type x3 -> x0, other arithmetic: 1.77 us -> none  [the longest x1 1.55 us: shards(): normed = rms_scale(rows_in, attn_gain).astype(BF16)]
    reduce_sum x2 -> x0, other arithmetic: 1.76 us -> none  [rms_scale(): jnp.mean(values * values, axis=-1, keepdims=True) + EPS]
    dynamic_slice x1 -> x0, local copies, waits for them, and re-layouts: 1.73 us -> none  [shards(): own_input = lax.dynamic_slice_in_dim(rows_in, own, row_dev)]
    concatenate x2 -> x0, other arithmetic: 1.51 us -> none  [the longest x1 0.83 us: rotary_tables(): jnp.concatenate([cosine, cosine], axis=1)]
    mul x0 -> x1, other arithmetic: none -> 1.24 us  [rotary_tables(): jnp.where(lane < half_width, -1.0, 1.0) * jnp.sin(angles)]
where the time goes in v3:
time: 105 us
  Pallas kernels  93.2 us (89%)
  local copies, waits for them, and re-layouts  9 us (9%)
  other arithmetic  2.27 us (2%)
    pallas_call x1, Pallas kernels, shards(): pl.pallas_call(layer_kernel, out_shape=jax.ShapeDtypeStruct((row_dev, wid...  93.2 us
    unnamed x6, local copies, waits for them, and re-layouts  6.01 us

profile of v3, /device:TPU:0, one launch (start us, length us, event | category | flops | bytes accessed | tf_op | source)
XLA Modules:
  0.0 104.5 jit_solution(6504835042889135539)
XLA Ops:
  0.0 0.0 copy-start
  0.0 0.8 dynamic_slice.16
  0.8 0.0 copy-done
  0.8 0.7 constant_dynamic-slice_fusion
  1.5 0.7 constant_dynamic-slice_fusion.2
  2.2 0.2 convert_reduce_fusion
  2.5 0.8 select_reduce_fusion.combine_ref
  3.3 0.8 copy.32.low_ref
  4.1 1.2 %fusion = (f32[256,64]{1,0:T(8,128)}, f32[256,64]{1,0:T(8,128)}) fusion(f32[256]{0:T(256)S(1)} %subtract_convert_fusion, f32[64]{0:T(128)S(1)} %get-tuple-element.7, f32[64]{0:T(128)S(1)} %get-tuple-element.8), kind=kLoop, calls=%fused_computation.5 | loop fusion | flops 32768 | bytes 132608 | tf_op jit(solution)/shard_map/mul | solution.py:30
  5.3 4.3 %copy.33.wd_hbm = bf16[2048,576]{1,0:T(8,128)(2,1)} copy(bf16[2048,576]{0,1:T(8,128)(2,1)} %param.23) | data formatting | bytes 4718592 | tf_op args[6]
  9.6 93.2 %shard_map.163 = bf16[64,2048]{1,0:T(8,128)(2,1)} custom-call(f32[256,64]{1,0:T(8,128)} %get-tuple-element.6.cos_ref, f32[256,64]{1,0:T(8,128)} %get-tuple-element.5.sin_ref, s32[256,1]{1,0:T(8,128)} %copy.32.low_ref, f32[1,2048]{1,0:T(1,128)} %bitcast.19, f32[1,512]{1,0:T(1,128)} %bitcast.21, f32[1,2048]{1,0:T(1,128)} %bitcast.20, ...), custom_call_target="tpu_custom_call" | custom-call | flops 14000000000 | bytes 25000000 | tf_op jit(solution)/shard_map/pallas_call | solution.py:407
  102.9 1.7 %copy.41 = bf16[1,64,2048]{2,1,0:T(8,128)(2,1)} copy(bf16[1,64,2048]{2,1,0:T(8,128)(2,1)} %bitcast.13) | data formatting | bytes 524288
  (5 shorter events, 0.0 us)
Async XLA Ops:
  0.0 0.8 copy-start

commit v4 on v3

--- a/solution.py
+++ b/solution.py
@@ -102,7 +102,9 @@
     normed[...] = rms_scale(x_in[...], attn_gain_ref[...]).astype(BF16)
     lead = pl.ds(pl.multiple_of(c * half, half), half)
     loads[1].wait()
-    compressed = jnp.dot(normed[lead, :], wd[...], preferred_element_type=F32)
+    compressed = lax.dot_general(
+        normed[lead, :], wd[...], (((1,), (1,)), ((), ())), preferred_element_type=F32
+    )
     keys[lead, :LATENT] = rms_scale(compressed[:, :LATENT], lat_gain_ref[...]).astype(BF16)
     keys[lead, LATENT:] = turned(
         compressed[:, LATENT:], cos_ref[lead, :], sin_ref[lead, :]
@@ -319,17 +321,17 @@
 
         start_core(k)
 
+        @pl.when(k + 1 < n_tok)
+        def _():
+            forward_core(k + 1)
+
+        @pl.when(k >= 1)
+        def _():
+            core_to_y(k)
+
         @pl.when(k >= 2)
         def _():
             to_ring(k - 1)
-
-        @pl.when(k + 1 < n_tok)
-        def _():
-            forward_core(k + 1)
-
-        @pl.when(k >= 1)
-        def _():
-            core_to_y(k)
 
     core_to_y(0)
     to_ring(jnp.int32(n_tok - 1))
@@ -398,7 +400,7 @@
         combining,
     ]
     weights = [
-        layer_input, w_kv_down, w_query, w_kv_up, w_out, w_shared_gate, w_shared_up, w_shared_down, w_expert_gate,
+        layer_input, w_kv_down.T, w_query, w_kv_up, w_out, w_shared_gate, w_shared_up, w_shared_down, w_expert_gate,
         w_expert_up, w_expert_down,
     ]
     held = [pltpu.VMEM((tok_dev, width), BF16)] * 2

time: 105 us -> 101 us (0.962)
  local copies, waits for them, and re-layouts: 9 us -> 4.67 us
    unnamed x6 -> x5, local copies, waits for them, and re-layouts: 6.01 us -> 1.68 us
where the time goes in v4:
time: 101 us
  Pallas kernels  94.2 us (93%)
  local copies, waits for them, and re-layouts  4.67 us (5%)
  other arithmetic  2.27 us (2%)
    pallas_call x1, Pallas kernels, shards(): pl.pallas_call(layer_kernel, out_shape=jax.ShapeDtypeStruct((row_dev, wid...  94.2 us

profile of v4, /device:TPU:0, one launch (start us, length us, event | category | flops | bytes accessed | tf_op | source)
XLA Modules:
  0.0 101.2 jit_solution(9551472355557844857)
XLA Ops:
  0.0 0.0 copy-start
  0.0 0.8 dynamic_slice.16
  0.8 0.0 copy-done
  0.8 0.7 constant_dynamic-slice_fusion
  1.5 0.7 constant_dynamic-slice_fusion.2
  2.2 0.2 convert_reduce_fusion
  2.5 0.8 select_reduce_fusion.combine_ref
  3.3 0.8 copy.29.low_ref
  4.1 1.2 %fusion = (f32[256,64]{1,0:T(8,128)}, f32[256,64]{1,0:T(8,128)}) fusion(f32[256]{0:T(256)S(1)} %subtract_convert_fusion, f32[64]{0:T(128)S(1)} %get-tuple-element.7, f32[64]{0:T(128)S(1)} %get-tuple-element.8), kind=kLoop, calls=%fused_computation.5 | loop fusion | flops 32768 | bytes 132608 | tf_op jit(solution)/shard_map/mul | solution.py:30
  5.3 94.2 %shard_map.163 = bf16[64,2048]{1,0:T(8,128)(2,1)} custom-call(f32[256,64]{1,0:T(8,128)} %get-tuple-element.6.cos_ref, f32[256,64]{1,0:T(8,128)} %get-tuple-element.5.sin_ref, s32[256,1]{1,0:T(8,128)} %copy.29.low_ref, f32[1,2048]{1,0:T(1,128)} %bitcast.21, f32[1,512]{1,0:T(1,128)} %bitcast.23, f32[1,2048]{1,0:T(1,128)} %bitcast.22, ...), custom_call_target="tpu_custom_call" | custom-call | flops 14000000000 | bytes 25000000 | tf_op jit(solution)/shard_map/pallas_call | solution.py:409
  99.5 1.7 %copy.37 = bf16[1,64,2048]{2,1,0:T(8,128)(2,1)} copy(bf16[1,64,2048]{2,1,0:T(8,128)(2,1)} %bitcast.14) | data formatting | bytes 524288
  (5 shorter events, 0.0 us)
Async XLA Ops:
  0.0 0.8 copy-start
